TPU v7x, 32 devices: a whole 2x2x4 slice. The times are simulated.
32 devices in a mesh: dp: 16 (over z, y, x), tensor: 2 (over core).
Axes of the slice: x: 2, y: 2, z: 4, core: 2. Of those that a mesh axis runs over, the one named last changes fastest.
Arguments:
- frames: bfloat16 [32768, 768], P('dp')
- cotangent: bfloat16 [32768, 768], P('dp'), may hold values from -6 to 6
- segment_ids: int32 [32768], P('dp'), may hold values from 0 to 9, as said below
- pad_mask: int32 [32768], P('dp'), may hold values from 0 to 1, as said below
- attention_weight: bfloat16 [4, 768, 768], P(None, None, 'tensor')
- feedforward_weight: bfloat16 [2, 768, 3072], P(None, None, 'tensor')
- head_bias: float32 [2, 2, 384], P(None, 'tensor'), may hold values from -3 to 3
- hidden_bias: float32 [2, 1536], P('tensor'), may hold values from -3 to 3
- norm_vectors: float32 [6, 768], replicated
- attention_first: float32 [4, 768, 768], P(None, 'dp', 'tensor')
- attention_second: float32 [4, 768, 768], P(None, 'dp', 'tensor')
- feedforward_first: float32 [2, 768, 3072], P(None, 'dp', 'tensor')
- feedforward_second: float32 [2, 768, 3072], P(None, 'dp', 'tensor')
- head_first: float32 [2, 2, 384], P(None, 'tensor', 'dp')
- head_second: float32 [2, 2, 384], P(None, 'tensor', 'dp')
- hidden_first: float32 [2, 1536], P('tensor', 'dp')
- hidden_second: float32 [2, 1536], P('tensor', 'dp')
- vector_first: float32 [6, 768], P(None, 'dp')
- vector_second: float32 [6, 768], P(None, 'dp')
Outputs:
- layer_output: bfloat16 [32768, 768], P('dp')
- input_gradient: float32 [32768, 768], P('dp')
- gradient_norm: float32 [], replicated
- new_attention_first: float32 [4, 768, 768], P(None, 'dp', 'tensor')
- new_attention_second: float32 [4, 768, 768], P(None, 'dp', 'tensor')
- new_attention: float32 [4, 768, 768], P(None, 'dp', 'tensor')
- new_feedforward_first: float32 [2, 768, 3072], P(None, 'dp', 'tensor')
- new_feedforward_second: float32 [2, 768, 3072], P(None, 'dp', 'tensor')
- new_feedforward: float32 [2, 768, 3072], P(None, 'dp', 'tensor')
- new_head_first: float32 [2, 2, 384], P(None, 'tensor', 'dp')
- new_head_second: float32 [2, 2, 384], P(None, 'tensor', 'dp')
- new_head_bias: float32 [2, 2, 384], P(None, 'tensor', 'dp')
- new_hidden_first: float32 [2, 1536], P('tensor', 'dp')
- new_hidden_second: float32 [2, 1536], P('tensor', 'dp')
- new_hidden_bias: float32 [2, 1536], P('tensor', 'dp')
- new_vector_first: float32 [6, 768], P(None, 'dp')
- new_vector_second: float32 [6, 768], P(None, 'dp')
- new_vectors: float32 [6, 768], P(None, 'dp')
Inputs may be any that keep to these rules, and one draw needn't show every extreme that they name: `segment_ids`: within each row of 1024 frames the ids start at 0 and never fall; each id covers one whole clip of 100 to 400 frames, and the padding at a row's end carries the id of the row's last clip; in every draw some row is packed with clips of exactly 100 frames. `pad_mask`: 1 on a row's frames up to the end of its last whole clip, 0 on the padding after it.
All inputs are finite; a program needn't handle non-finite values.
Results may differ from a plain program's by a relative error of at most 0.02.
Values may be sent and summed in bfloat16 or wider, within the bound.
No kernel may reach another device: no remote copies, remote signals or barrier semaphores. Data moves between devices by JAX's collectives and lax.ppermute only.
A program may use at most 192 MiB of HBM per device.

v0:
```python
import jax
import jax.numpy as jnp
from jax import lax
from jax.sharding import PartitionSpec as P

HD = 64
SEQ = 1024
STEP = 10


def layer_norm(value, gain, shift):
    center = value - jnp.mean(value, axis=-1, keepdims=True)
    inv_std = lax.rsqrt(jnp.mean(center * center, axis=-1, keepdims=True) + 1e-05)
    normed = center * inv_std
    return (normed * gain + shift, normed, inv_std)


def norm_back(grad, normed, inv_std, gain):
    scaled = grad * gain
    mean_one = jnp.mean(scaled, axis=-1, keepdims=True)
    mean_two = jnp.mean(scaled * normed, axis=-1, keepdims=True)
    back = inv_std * (scaled - mean_one - normed * mean_two)
    return (back, jnp.sum(grad * normed, axis=0), jnp.sum(grad, axis=0))


def gelu_exact(value):
    return jax.nn.gelu(value, approximate=False)


def masked_scores(piece, keys, seg_block, seg_row, valid_row):
    scores = jnp.einsum("qhd,khd->hqk", piece, keys, preferred_element_type=jnp.float32) * HD ** (
        -0.5
    )
    allowed = (seg_block[:, None] == seg_row[None, :]) & (valid_row[None, :] == 1)
    return jnp.where(allowed[None], scores, -1000000000.0)


def attention_forward(query, keys, values, seg_row, valid_row):
    block = min(512, SEQ)
    outputs = []
    totals = []
    for begin in range(0, SEQ, block):
        piece = query[begin : begin + block]
        scores = masked_scores(piece, keys, seg_row[begin : begin + block], seg_row, valid_row)
        top = jnp.max(scores, axis=-1, keepdims=True)
        expo = jnp.exp(scores - top)
        total = jnp.sum(expo, axis=-1, keepdims=True)
        probs = (expo / total).astype(jnp.bfloat16)
        outputs.append(
            jnp.einsum("hqk,khd->qhd", probs, values, preferred_element_type=jnp.float32)
        )
        totals.append((top + jnp.log(total))[..., 0])
    return (jnp.concatenate(outputs, axis=0), jnp.concatenate(totals, axis=1))


def attention_backward(query, keys, values, seg_row, valid_row, log_totals, out_grad):
    block = min(512, SEQ)
    scale = HD ** (-0.5)
    key_grad = jnp.zeros(keys.shape, jnp.float32)
    value_grad = jnp.zeros(values.shape, jnp.float32)
    query_grads = []
    for begin in range(0, SEQ, block):
        piece = query[begin : begin + block]
        scores = masked_scores(piece, keys, seg_row[begin : begin + block], seg_row, valid_row)
        probs = jnp.exp(scores - log_totals[:, begin : begin + block, None])
        probs_low = probs.astype(jnp.bfloat16)
        grad_piece = out_grad[begin : begin + block]
        value_grad = value_grad + jnp.einsum(
            "hqk,qhd->khd", probs_low, grad_piece, preferred_element_type=jnp.float32
        )
        prob_grad = jnp.einsum(
            "qhd,khd->hqk", grad_piece, values, preferred_element_type=jnp.float32
        )
        score_grad = (
            probs * (prob_grad - jnp.sum(probs * prob_grad, axis=-1, keepdims=True))
        ).astype(jnp.bfloat16)
        query_grads.append(
            jnp.einsum("hqk,khd->qhd", score_grad, keys, preferred_element_type=jnp.float32) * scale
        )
        key_grad = (
            key_grad
            + jnp.einsum("hqk,qhd->khd", score_grad, piece, preferred_element_type=jnp.float32)
            * scale
        )
    return (jnp.concatenate(query_grads, axis=0), key_grad, value_grad)


def adam_step(grad, first, second, weight, factor, rate, decay):
    clipped = grad * factor
    first_new = 0.9 * first + 0.1 * clipped
    second_new = 0.999 * second + 0.001 * clipped * clipped
    mean_hat = first_new / (1.0 - 0.9**STEP)
    var_hat = second_new / (1.0 - 0.999**STEP)
    weight_new = weight - rate * (mean_hat / (jnp.sqrt(var_hat) + 1e-08) + decay * weight)
    return (first_new, second_new, weight_new)


def local(
    frames,
    cotangent,
    segment_ids,
    pad_mask,
    attention_weight,
    feedforward_weight,
    head_bias,
    hidden_bias,
    norm_vectors,
    attention_first,
    attention_second,
    feedforward_first,
    feedforward_second,
    head_first,
    head_second,
    hidden_first,
    hidden_second,
    vector_first,
    vector_second,
):
    width = frames.shape[1]
    micro = frames.shape[0] // SEQ
    tensor_count = lax.axis_size("tensor")
    weights = (attention_weight, feedforward_weight, head_bias, hidden_bias)
    att_w, ffw_w, head_w, hidden_w = weights
    head_cols = att_w.shape[2]
    unit_cols = ffw_w.shape[2]
    local_heads = head_cols // HD
    head_shape = (SEQ, local_heads, HD)
    head_flat = head_w.reshape(2, head_cols)
    hidden_flat = hidden_w.reshape(unit_cols)

    def micro_pass(row, cot_row, seg_row, valid_row):
        row32 = row.astype(jnp.float32)
        projected = jnp.einsum("sd,kde->kse", row, att_w[:3], preferred_element_type=jnp.float32)
        query = (projected[0] + head_flat[0]).astype(jnp.bfloat16).reshape(head_shape)
        keys = projected[1].astype(jnp.bfloat16).reshape(head_shape)
        values = (projected[2] + head_flat[1]).astype(jnp.bfloat16).reshape(head_shape)
        attended, log_totals = attention_forward(query, keys, values, seg_row, valid_row)
        mixed = attended.reshape(SEQ, head_cols).astype(jnp.bfloat16)
        partial_value = jnp.einsum(
            "sc,dc->sd", mixed, att_w[3], preferred_element_type=jnp.float32
        ).astype(jnp.bfloat16)
        attn_total = lax.psum(partial_value, "tensor").astype(jnp.float32)
        first = row32 + attn_total + norm_vectors[0]
        first_norm, normed_one, inv_one = layer_norm(first, norm_vectors[1], norm_vectors[2])
        first_low = first_norm.astype(jnp.bfloat16)
        up_pre = jnp.dot(first_low, ffw_w[0], preferred_element_type=jnp.float32) + hidden_flat
        act_low = gelu_exact(up_pre).astype(jnp.bfloat16)
        partial_two = jnp.einsum(
            "sh,dh->sd", act_low, ffw_w[1], preferred_element_type=jnp.float32
        ).astype(jnp.bfloat16)
        ffn_total = lax.psum(partial_two, "tensor").astype(jnp.float32)
        second = first_norm + ffn_total + norm_vectors[3]
        result, normed_two, inv_two = layer_norm(second, norm_vectors[4], norm_vectors[5])
        grad_out = cot_row.astype(jnp.float32) * valid_row[:, None].astype(jnp.float32)
        grad_second, gain_two_grad, shift_two_grad = norm_back(
            grad_out, normed_two, inv_two, norm_vectors[4]
        )
        down_bias_grad = jnp.sum(grad_second, axis=0)
        second_low = grad_second.astype(jnp.bfloat16)
        down_grad = jnp.einsum("sd,sh->dh", second_low, act_low, preferred_element_type=jnp.float32)
        act_grad = jnp.einsum("sd,dh->sh", second_low, ffw_w[1], preferred_element_type=jnp.float32)
        unused, gelu_back = jax.vjp(gelu_exact, up_pre)
        up_grad = gelu_back(act_grad)[0].astype(jnp.bfloat16)
        hidden_grad = jnp.sum(up_grad.astype(jnp.float32), axis=0)
        up_weight_grad = jnp.einsum(
            "sd,sh->dh", first_low, up_grad, preferred_element_type=jnp.float32
        )
        norm_part = jnp.einsum("sh,dh->sd", up_grad, ffw_w[0], preferred_element_type=jnp.float32)
        first_norm_grad = (
            lax.psum(norm_part.astype(jnp.bfloat16), "tensor").astype(jnp.float32) + grad_second
        )
        grad_first, gain_one_grad, shift_one_grad = norm_back(
            first_norm_grad, normed_one, inv_one, norm_vectors[1]
        )
        out_bias_grad = jnp.sum(grad_first, axis=0)
        first_grad_low = grad_first.astype(jnp.bfloat16)
        out_weight_grad = jnp.einsum(
            "sd,sc->dc", first_grad_low, mixed, preferred_element_type=jnp.float32
        )
        mixed_grad = jnp.einsum(
            "sd,dc->sc", first_grad_low, att_w[3], preferred_element_type=jnp.float32
        ).astype(jnp.bfloat16)
        query_grad, key_grad, value_grad = attention_backward(
            query, keys, values, seg_row, valid_row, log_totals, mixed_grad.reshape(head_shape)
        )
        triple_grad = (
            jnp.stack([query_grad, key_grad, value_grad])
            .reshape(3, SEQ, head_cols)
            .astype(jnp.bfloat16)
        )
        triple_weight_grad = jnp.einsum(
            "sd,kse->kde", row, triple_grad, preferred_element_type=jnp.float32
        )
        bias_sums = jnp.sum(triple_grad.astype(jnp.float32), axis=1)
        head_grad = jnp.stack([bias_sums[0], bias_sums[2]]).reshape(head_w.shape)
        input_part = jnp.einsum(
            "kse,kde->sd", triple_grad, att_w[:3], preferred_element_type=jnp.float32
        )
        input_row = (
            lax.psum(input_part.astype(jnp.bfloat16), "tensor").astype(jnp.float32) + grad_first
        )
        attention_grad = jnp.concatenate([triple_weight_grad, out_weight_grad[None]], axis=0)
        feedforward_grad = jnp.stack([up_weight_grad, down_grad])
        vector_grad = jnp.stack(
            [
                out_bias_grad,
                gain_one_grad,
                shift_one_grad,
                down_bias_grad,
                gain_two_grad,
                shift_two_grad,
            ]
        )
        grads = (
            attention_grad,
            feedforward_grad,
            head_grad,
            hidden_grad.reshape(hidden_w.shape),
            vector_grad,
        )
        return (result.astype(jnp.bfloat16), input_row, grads)

    blocks = (
        frames.reshape(micro, SEQ, width),
        cotangent.reshape(micro, SEQ, width),
        segment_ids.reshape(micro, SEQ),
        pad_mask.reshape(micro, SEQ),
    )
    local_cols = attention_weight.shape[2]
    local_units = feedforward_weight.shape[2]
    init = (
        jnp.zeros((4, width, local_cols), jnp.float32),
        jnp.zeros((2, width, local_units), jnp.float32),
        jnp.zeros((2, 1, local_cols), jnp.float32),
        jnp.zeros((1, local_units), jnp.float32),
        jnp.zeros((6, width), jnp.float32),
    )

    def step_heads(carry, block):
        out_row, input_row, grads = micro_pass(block[0], block[1], block[2], block[3])
        carry = jax.tree.map(jnp.add, carry, grads)
        return (carry, (out_row, input_row))

    totals, outputs = lax.scan(step_heads, init, blocks)
    shards = (
        lax.psum_scatter(totals[0], "dp", scatter_dimension=1, tiled=True),
        lax.psum_scatter(totals[1], "dp", scatter_dimension=1, tiled=True),
        lax.psum_scatter(totals[2], "dp", scatter_dimension=2, tiled=True),
        lax.psum_scatter(totals[3], "dp", scatter_dimension=1, tiled=True),
        lax.psum_scatter(totals[4], "dp", scatter_dimension=1, tiled=True),
    )
    layer_output = outputs[0].reshape(micro * SEQ, width)
    input_gradient = outputs[1].reshape(micro * SEQ, width)
    attention_shard, feedforward_shard, head_shard, hidden_shard, vector_shard = shards
    split_squares = (
        jnp.sum(attention_shard * attention_shard)
        + jnp.sum(feedforward_shard * feedforward_shard)
        + jnp.sum(head_shard * head_shard)
        + jnp.sum(hidden_shard * hidden_shard)
    )
    shared_squares = jnp.sum(vector_shard * vector_shard) / tensor_count
    total_squares = lax.psum(split_squares + shared_squares, ("dp", "tensor"))
    gradient_norm = jnp.sqrt(total_squares)
    factor = jnp.minimum(1.0, 1.0 / (gradient_norm + 1e-06))
    dp_index = lax.axis_index("dp")
    rows_owned = attention_shard.shape[1]
    old_attention = lax.dynamic_slice_in_dim(
        attention_weight, dp_index * rows_owned, rows_owned, 1
    ).astype(jnp.float32)
    old_feedforward = lax.dynamic_slice_in_dim(
        feedforward_weight, dp_index * rows_owned, rows_owned, 1
    ).astype(jnp.float32)
    head_owned = head_shard.shape[2]
    old_head = lax.dynamic_slice_in_dim(head_bias, dp_index * head_owned, head_owned, 2)
    hidden_owned = hidden_shard.shape[1]
    old_hidden = lax.dynamic_slice_in_dim(hidden_bias, dp_index * hidden_owned, hidden_owned, 1)
    old_vectors = lax.dynamic_slice_in_dim(norm_vectors, dp_index * rows_owned, rows_owned, 1)
    att = adam_step(
        attention_shard, attention_first, attention_second, old_attention, factor, 0.05, 0.01
    )
    ffw = adam_step(
        feedforward_shard,
        feedforward_first,
        feedforward_second,
        old_feedforward,
        factor,
        0.05,
        0.01,
    )
    hed = adam_step(head_shard, head_first, head_second, old_head, factor, 0.5, 0.0)
    hid = adam_step(hidden_shard, hidden_first, hidden_second, old_hidden, factor, 0.5, 0.0)
    vec = adam_step(vector_shard, vector_first, vector_second, old_vectors, factor, 0.5, 0.0)
    return (
        layer_output,
        input_gradient,
        gradient_norm,
        att[0],
        att[1],
        att[2],
        ffw[0],
        ffw[1],
        ffw[2],
        hed[0],
        hed[1],
        hed[2],
        hid[0],
        hid[1],
        hid[2],
        vec[0],
        vec[1],
        vec[2],
    )


def solution(mesh):
    placed = (
        P("dp", None),
        P("dp", None),
        P("dp"),
        P("dp"),
        P(None, None, "tensor"),
        P(None, None, "tensor"),
        P(None, "tensor", None),
        P("tensor", None),
        P(),
        P(None, "dp", "tensor"),
        P(None, "dp", "tensor"),
        P(None, "dp", "tensor"),
        P(None, "dp", "tensor"),
        P(None, "tensor", "dp"),
        P(None, "tensor", "dp"),
        P("tensor", "dp"),
        P("tensor", "dp"),
        P(None, "dp"),
        P(None, "dp"),
    )
    return jax.shard_map(
        local,
        mesh=mesh,
        in_specs=placed,
        out_specs=(
            P("dp", None),
            P("dp", None),
            P(),
            P(None, "dp", "tensor"),
            P(None, "dp", "tensor"),
            P(None, "dp", "tensor"),
            P(None, "dp", "tensor"),
            P(None, "dp", "tensor"),
            P(None, "dp", "tensor"),
            P(None, "tensor", "dp"),
            P(None, "tensor", "dp"),
            P(None, "tensor", "dp"),
            P("tensor", "dp"),
            P("tensor", "dp"),
            P("tensor", "dp"),
            P(None, "dp"),
            P(None, "dp"),
            P(None, "dp"),
        ),
        check_vma=False,
    )
```

profile of v0, /device:TPU:0, one launch (start us, length us, event | category | flops | bytes accessed | tf_op | source)
XLA Modules:
  0.0 1153.9 jit_solution(5332410703892356605)
XLA Ops:
  15.6 503.8 %while.23 = (s32[]{:T(128)}, f32[4,768,384]{1,2,0:T(8,128)}, f32[2,768,1536]{2,1,0:T(8,128)}, f32[2,1,384]{2,1,0:T(1,128)}, f32[1,1536]{1,0:T(1,128)S(1)}, /*ind...) while((s32[]{:T(128)}, f32[4,768,384]{1,2,0:T(8,128)}, ...), condition=%wide.region_27.28_spmd.clone, body=%wide.region_0.27_spmd.clone.sunk | while | flops 26934243328 | bytes 962634240 | solution.py:244
  52.0 22.0 %all-reduce.6.cloned.1.call-done = bf16[1024,768]{1,0:T(8,128)(2,1)} async-done(((bf16[1024,768]{1,0:T(8,128)(2,1)}), bf16[1024,768]{1,0:T(8,128)(2,1)}) %all-reduce.6.cloned.1.call-update) | async-done | bytes 1572880 | tf_op jit(solution)/shard_map/while/body/eval_jaxpr/psum | solution.py:142
  78.9 20.5 %multiply_convert_fusion.8 = (bf16[1024,1536]{1,0:T(8,128)(2,1)S(1)}, f32[1024,1536]{1,0:T(8,128)}, f32[1024,1536]{1,0:T(8,128)}) fusion(f32[1536]{0:T(1024)S(1)} %reduce.26, bf16[2,768,1536]{2,1,0:T(8,128)(2,1)} %get-tuple-element.552, f32[768]{0:T(1024)S(1)} %get-tuple-element.463, f32[768]{0:T(1024)S(1)} %get-tuple-element.464, ...), kind=kOutput, calls=%fused_computation.24.clone.1 | convolution fusion | flops 2526806016 | bytes 21257220 | tf_op jit(solution)/shard_map/while/body/eval_jaxpr/dot_general | solution.py:146
  106.2 20.4 %all-reduce.8.cloned.1.call-done = bf16[1024,768]{1,0:T(8,128)(2,1)} async-done(((bf16[1024,768]{1,0:T(8,128)(2,1)}), bf16[1024,768]{1,0:T(8,128)(2,1)}) %all-reduce.8.cloned.1.call-update) | async-done | bytes 1572880 | tf_op jit(solution)/shard_map/while/body/eval_jaxpr/psum | solution.py:151
  139.8 6.6 convert_reduce_fusion.4
  151.9 8.1 convolution_bitcast_fusion.14
  162.2 10.0 maximum_add_fusion.5
  184.4 6.2 multiply_reduce_fusion.20
  190.6 10.0 multiply_convert_fusion.9
  200.6 5.8 fusion.258
  213.7 7.2 multiply_reduce_fusion.21
  224.4 6.7 multiply_convert_fusion.10
  249.5 13.2 %all-reduce.12.cloned.1.call-done = bf16[1024,768]{1,0:T(8,128)(2,1)} async-done(((bf16[1024,768]{1,0:T(8,128)(2,1)}), bf16[1024,768]{1,0:T(8,128)(2,1)}) %all-reduce.12.cloned.1.call-update) | async-done | bytes 1572880 | tf_op jit(solution)/shard_map/while/body/eval_jaxpr/psum | solution.py:200
  302.9 20.2 %all-reduce.6.cloned.1.call-done = bf16[1024,768]{1,0:T(8,128)(2,1)} async-done(((bf16[1024,768]{1,0:T(8,128)(2,1)}), bf16[1024,768]{1,0:T(8,128)(2,1)}) %all-reduce.6.cloned.1.call-update) | async-done | bytes 1572880 | tf_op jit(solution)/shard_map/while/body/eval_jaxpr/psum | solution.py:142
  328.1 20.5 %multiply_convert_fusion.8 = (bf16[1024,1536]{1,0:T(8,128)(2,1)S(1)}, f32[1024,1536]{1,0:T(8,128)}, f32[1024,1536]{1,0:T(8,128)}) fusion(f32[1536]{0:T(1024)S(1)} %reduce.26, bf16[2,768,1536]{2,1,0:T(8,128)(2,1)} %get-tuple-element.552, f32[768]{0:T(1024)S(1)} %get-tuple-element.463, f32[768]{0:T(1024)S(1)} %get-tuple-element.464, ...), kind=kOutput, calls=%fused_computation.24.clone.1 | convolution fusion | flops 2526806016 | bytes 21257220 | tf_op jit(solution)/shard_map/while/body/eval_jaxpr/dot_general | solution.py:146
  355.3 20.4 %all-reduce.8.cloned.1.call-done = bf16[1024,768]{1,0:T(8,128)(2,1)} async-done(((bf16[1024,768]{1,0:T(8,128)(2,1)}), bf16[1024,768]{1,0:T(8,128)(2,1)}) %all-reduce.8.cloned.1.call-update) | async-done | bytes 1572880 | tf_op jit(solution)/shard_map/while/body/eval_jaxpr/psum | solution.py:151
  389.0 6.6 convert_reduce_fusion.4
  401.0 8.1 convolution_bitcast_fusion.14
  411.4 12.5 %maximum_add_fusion.5 = f32[2,768,1536]{2,1,0:T(8,128)} fusion(f32[1,768,1536]{2,1,0:T(8,128)} %convolution_bitcast_fusion.13, f32[1,768,1536]{2,1,0:T(8,128)} %convolution_bitcast_fusion.14, f32[2,768,1536]{2,1,0:T(8,128)} %get-tuple-element.519, pred[]{:T(512)S(6)} %compare.3), kind=kLoop, calls=%fused_computation.17.clone.1 | loop fusion | flops 7077888 | bytes 28311552 | tf_op jit(solution)/shard_map/while/body/eval_jaxpr/add | solution.py:241
  434.5 6.2 multiply_reduce_fusion.20
  440.7 10.0 multiply_convert_fusion.9
  450.7 5.8 fusion.258
  463.8 7.2 multiply_reduce_fusion.21
  474.5 6.9 multiply_convert_fusion.10
  502.7 10.4 all-reduce.12.cloned.1.call-done
  522.5 6.1 copy.46
  530.6 42.1 %all-reduce = f32[2,1,384]{2,1,0:T(1,128)S(1)} all-reduce(f32[2,1,384]{2,1,0:T(1,128)S(1)} %copy-done.39), channel_id=4, replica_groups=mesh['dp'=16,'tensor'=2] {'dp'}, use_global_device_ids=true, to_apply=%region_32.33.clone | all-reduce | flops 768 | bytes 6144
  573.4 75.1 %reduce-scatter.14.cloned.1.call-done = f32[96,1]{1,0:T(8,128)} async-done(((f32[1536,1]{1,0:T(8,128)}), f32[96,1]{1,0:T(8,128)}) %reduce-scatter.14.cloned.1.call-update) | async-done | bytes 400
  649.9 124.2 %reduce-scatter.16.cloned.1.call-done = f32[48,6]{1,0:T(8,128)} async-done(((f32[768,6]{1,0:T(8,128)}), f32[48,6]{1,0:T(8,128)}) %reduce-scatter.16.cloned.1.call-update) | async-done | bytes 1168
  776.2 140.6 %reduce-scatter.10.cloned.1.call-done = f32[4,48,384]{2,1,0:T(8,128)} async-done(((f32[4,768,384]{2,1,0:T(8,128)}), f32[4,48,384]{2,1,0:T(8,128)}) %reduce-scatter.10.cloned.1.call-update) | async-done | bytes 294928 | tf_op jit(solution)/shard_map/reduce_scatter | solution.py:246
  918.5 173.7 %reduce-scatter.12.cloned.1.call-done = f32[2,48,1536]{2,1,0:T(8,128)} async-done(((f32[2,768,1536]{2,1,0:T(8,128)}), f32[2,48,1536]{2,1,0:T(8,128)}) %reduce-scatter.12.cloned.1.call-update) | async-done | bytes 589840 | tf_op jit(solution)/shard_map/reduce_scatter | solution.py:247
  1096.6 39.5 %psum.35 = f32[]{:T(128)} all-reduce(f32[]{:T(128)S(6)} %add.270), channel_id=1, replica_groups=mesh['dp'=16,'tensor'=2] {'dp','tensor'}, use_global_device_ids=true, to_apply=%region_38.39 | all-reduce | flops 1 | bytes 8 | tf_op jit(solution)/shard_map/psum | solution.py:262
  (426 shorter events, 254.4 us)
Async XLA Ops:
  15.7 58.3 %all-reduce.6.cloned.1.call-start = ((), (), s32[]{:S(2)}) async-start(), calls=%async_computation.8 | async-start | bytes 3145728 | tf_op jit(solution)/shard_map/while/body/eval_jaxpr/psum | solution.py:142
  26.2 16.2 %copy-start.10 = (bf16[1024,6,64]{0,2,1:T(8,128)(2,1)}, bf16[1024,6,64]{0,2,1:T(8,128)(2,1)S(1)}, u32[]{:S(2)}) copy-start(bf16[1024,6,64]{0,2,1:T(8,128)(2,1)S(1)} %add_convert_fusion.6) | copy-start | bytes 2359300 | tf_op jit(solution)/shard_map/while
  50.7 75.8 %all-reduce.8.cloned.1.call-start = ((), (), s32[]{:S(2)}) async-start(), calls=%async_computation.9 | async-start | bytes 3145728 | tf_op jit(solution)/shard_map/while/body/eval_jaxpr/psum | solution.py:151
  74.0 27.1 %slice-start.7 = ((s8[4718592]{0:T(1024)(128)(4,1)}), s8[4194304]{0:T(1024)(128)(4,1)S(1)}, s32[]{:S(2)}) async-start(s8[4718592]{0:T(1024)(128)(4,1)} %bitcast.329), calls=%async_computation.19 | async-start | bytes 8388608 | tf_op jit(solution)/shard_map/while
  78.9 22.2 %slice-start.8 = ((s8[4718592]{0:T(1024)(128)(4,1)}), s8[524288]{0:T(1024)(128)(4,1)S(1)}, s32[]{:S(2)}) async-start(s8[4718592]{0:T(1024)(128)(4,1)} %bitcast.329), calls=%async_computation.20 | async-start | bytes 1048576 | tf_op jit(solution)/shard_map/while
  104.8 68.7 %all-reduce.10.cloned.1.call-start = ((), (), s32[]{:S(2)}) async-start(), calls=%async_computation.10 | async-start | bytes 3145728 | tf_op jit(solution)/shard_map/while/body/eval_jaxpr/psum | solution.py:170
  151.8 110.9 %all-reduce.12.cloned.1.call-start = ((), (), s32[]{:S(2)}) async-start(), calls=%async_computation.11 | async-start | bytes 3145728 | tf_op jit(solution)/shard_map/while/body/eval_jaxpr/psum | solution.py:200
  190.6 19.9 %slice-start.3 = ((s8[12582912]{0:T(1024)(128)(4,1)}), s8[4194304]{0:T(1024)(128)(4,1)S(1)}, s32[]{:S(2)}) async-start(s8[12582912]{0:T(1024)(128)(4,1)} %bitcast.290), calls=%async_computation.15 | async-start | bytes 8388608 | tf_op jit(solution)/shard_map/while
  190.6 19.9 %slice-start.4 = ((s8[12582912]{0:T(1024)(128)(4,1)}), s8[4194304]{0:T(1024)(128)(4,1)S(1)}, s32[]{:S(2)}) async-start(s8[12582912]{0:T(1024)(128)(4,1)} %bitcast.290), calls=%async_computation.16 | async-start | bytes 8388608 | tf_op jit(solution)/shard_map/while
  266.3 56.9 %all-reduce.6.cloned.1.call-start = ((), (), s32[]{:S(2)}) async-start(), calls=%async_computation.8 | async-start | bytes 3145728 | tf_op jit(solution)/shard_map/while/body/eval_jaxpr/psum | solution.py:142
  276.9 16.2 %copy-start.10 = (bf16[1024,6,64]{0,2,1:T(8,128)(2,1)}, bf16[1024,6,64]{0,2,1:T(8,128)(2,1)S(1)}, u32[]{:S(2)}) copy-start(bf16[1024,6,64]{0,2,1:T(8,128)(2,1)S(1)} %add_convert_fusion.6) | copy-start | bytes 2359300 | tf_op jit(solution)/shard_map/while
  301.4 74.3 %all-reduce.8.cloned.1.call-start = ((), (), s32[]{:S(2)}) async-start(), calls=%async_computation.9 | async-start | bytes 3145728 | tf_op jit(solution)/shard_map/while/body/eval_jaxpr/psum | solution.py:151
  323.1 27.1 %slice-start.7 = ((s8[4718592]{0:T(1024)(128)(4,1)}), s8[4194304]{0:T(1024)(128)(4,1)S(1)}, s32[]{:S(2)}) async-start(s8[4718592]{0:T(1024)(128)(4,1)} %bitcast.329), calls=%async_computation.19 | async-start | bytes 8388608 | tf_op jit(solution)/shard_map/while
  328.1 22.2 %slice-start.8 = ((s8[4718592]{0:T(1024)(128)(4,1)}), s8[524288]{0:T(1024)(128)(4,1)S(1)}, s32[]{:S(2)}) async-start(s8[4718592]{0:T(1024)(128)(4,1)} %bitcast.329), calls=%async_computation.20 | async-start | bytes 1048576 | tf_op jit(solution)/shard_map/while
  354.0 69.9 %all-reduce.10.cloned.1.call-start = ((), (), s32[]{:S(2)}) async-start(), calls=%async_computation.10 | async-start | bytes 3145728 | tf_op jit(solution)/shard_map/while/body/eval_jaxpr/psum | solution.py:170
  401.0 112.1 %all-reduce.12.cloned.1.call-start = ((), (), s32[]{:S(2)}) async-start(), calls=%async_computation.11 | async-start | bytes 3145728 | tf_op jit(solution)/shard_map/while/body/eval_jaxpr/psum | solution.py:200
  440.7 19.9 %slice-start.3 = ((s8[12582912]{0:T(1024)(128)(4,1)}), s8[4194304]{0:T(1024)(128)(4,1)S(1)}, s32[]{:S(2)}) async-start(s8[12582912]{0:T(1024)(128)(4,1)} %bitcast.290), calls=%async_computation.15 | async-start | bytes 8388608 | tf_op jit(solution)/shard_map/while
  440.7 19.9 %slice-start.4 = ((s8[12582912]{0:T(1024)(128)(4,1)}), s8[4194304]{0:T(1024)(128)(4,1)S(1)}, s32[]{:S(2)}) async-start(s8[12582912]{0:T(1024)(128)(4,1)} %bitcast.290), calls=%async_computation.16 | async-start | bytes 8388608 | tf_op jit(solution)/shard_map/while
  519.4 129.0 %reduce-scatter.14.cloned.1.call-start = ((), (), s32[]{:S(2)}) async-start(), calls=%async_computation.6 | async-start | bytes 835584
  520.7 253.4 %reduce-scatter.16.cloned.1.call-start = ((), (), s32[]{:S(2)}) async-start(), calls=%async_computation.7 | async-start | bytes 417792
  522.4 394.4 %reduce-scatter.10.cloned.1.call-start = ((), (), s32[]{:S(2)}) async-start(), calls=%async_computation.4 | async-start | bytes 5013504 | tf_op jit(solution)/shard_map/reduce_scatter | solution.py:246
  528.6 563.6 %reduce-scatter.12.cloned.1.call-start = ((), (), s32[]{:S(2)}) async-start(), calls=%async_computation.5 | async-start | bytes 10027008 | tf_op jit(solution)/shard_map/reduce_scatter | solution.py:247
  528.7 608.2 %copy-start.42 = (f32[2,1,24]{2,1,0:T(1,128)S(1)}, f32[2,1,24]{2,1,0:T(1,128)}, u32[]{:S(2)}) copy-start(f32[2,1,24]{2,1,0:T(1,128)} %param.35) | copy-start | bytes 580
  528.7 608.2 %copy-start.43 = (f32[2,1,24]{2,1,0:T(1,128)S(1)}, f32[2,1,24]{2,1,0:T(1,128)}, u32[]{:S(2)}) copy-start(f32[2,1,24]{2,1,0:T(1,128)} %param.34) | copy-start | bytes 580
  528.7 609.5 %copy-start.44 = (f32[1,96]{1,0:T(1,128)S(1)}, f32[1,96]{1,0:T(1,128)}, u32[]{:S(2)}) copy-start(f32[1,96]{1,0:T(1,128)} %param.37) | copy-start | bytes 1156
  528.7 609.5 %copy-start.45 = (f32[1,96]{1,0:T(1,128)S(1)}, f32[1,96]{1,0:T(1,128)}, u32[]{:S(2)}) copy-start(f32[1,96]{1,0:T(1,128)} %param.36) | copy-start | bytes 1156
  528.7 610.1 %copy-start.40 = (f32[6,48]{1,0:T(8,128)S(1)}, f32[6,48]{1,0:T(8,128)}, u32[]{:S(2)}) copy-start(f32[6,48]{1,0:T(8,128)} %param.39) | copy-start | bytes 3460
  528.7 610.1 %copy-start.41 = (f32[6,48]{1,0:T(8,128)S(1)}, f32[6,48]{1,0:T(8,128)}, u32[]{:S(2)}) copy-start(f32[6,48]{1,0:T(8,128)} %param.38) | copy-start | bytes 3460
  528.7 611.4 %copy-start.33 = (f32[4,48,384]{2,1,0:T(8,128)S(1)}, f32[4,48,384]{2,1,0:T(8,128)}, u32[]{:S(2)}) copy-start(f32[4,48,384]{2,1,0:T(8,128)} %param.31) | copy-start | bytes 884740
  528.7 611.4 %copy-start.34 = (f32[4,48,384]{2,1,0:T(8,128)S(1)}, f32[4,48,384]{2,1,0:T(8,128)}, u32[]{:S(2)}) copy-start(f32[4,48,384]{2,1,0:T(8,128)} %param.30) | copy-start | bytes 884740
  529.3 613.0 %copy-start.31 = (f32[2,48,1536]{2,1,0:T(8,128)S(1)}, f32[2,48,1536]{2,1,0:T(8,128)}, u32[]{:S(2)}) copy-start(f32[2,48,1536]{2,1,0:T(8,128)} %param.33) | copy-start | bytes 1769476
  529.3 613.0 %copy-start.32 = (f32[2,48,1536]{2,1,0:T(8,128)S(1)}, f32[2,48,1536]{2,1,0:T(8,128)}, u32[]{:S(2)}) copy-start(f32[2,48,1536]{2,1,0:T(8,128)} %param.32) | copy-start | bytes 1769476
  (93 other events, 476.8 us)
Sparse Core Ops, SparseCore 0:
  50.8 23.0 all-reduce.5
  104.9 21.5 all-reduce.7
  151.9 21.5 all-reduce.9
  241.1 21.5 all-reduce.11
  301.5 21.5 all-reduce.5
  354.1 21.5 all-reduce.7
  401.1 21.5 all-reduce.9
  491.4 21.5 all-reduce.11
Sparse Core Ops, SparseCore 1:
  524.6 123.8 reduce-scatter.13
  653.5 120.5 reduce-scatter.15
  780.0 136.8 reduce-scatter.9
  922.5 169.6 reduce-scatter.11
where the time goes:
time: 1160 us; the launch traced here: 1150 us
  waiting for transfers between devices  622 us (54%)
  matrix products  224 us (19%)
  other arithmetic  144 us (12%)
  blocking collectives  81.6 us (7%)
  local copies, waits for them, and re-layouts  54.1 us (5%)
  between operations  21.9 us (2%)
    unnamed x6, waiting for transfers between devices  200 us
    reduce_scatter x1, waiting for transfers between devices, local(): lax.psum_scatter(totals[1], 'dp', scatter_dimension=1, tiled=True)  174 us
    reduce_scatter x1, waiting for transfers between devices, local(): lax.psum_scatter(totals[0], 'dp', scatter_dimension=1, tiled=True)  141 us
    psum x2, waiting for transfers between devices, micro_pass(): attn_total = lax.psum(partial_value, 'tensor').astype(jnp.float32)  42.2 us
    unnamed x1, blocking collectives  42.1 us
    dot_general x2, matrix products, micro_pass(): jnp.dot(first_low, ffw_w[0], preferred_element_type=jnp.float32)  41 us
    psum x2, waiting for transfers between devices, micro_pass(): ffn_total = lax.psum(partial_two, 'tensor').astype(jnp.float32)  40.8 us
    psum x1, blocking collectives, local(): total_squares = lax.psum(split_squares + shared_squares, ('dp', 'tensor'))  39.5 us
  transfers between devices with their start and end apart: 12, of which 11 were waited for; matrix products, arithmetic and copies ran while one was open for 7% of the time, Pallas kernels for 0%

commit v1 on v0

v1 whole, which is shorter than its diff:
```python
import functools

import jax
import jax.numpy as jnp
from jax import lax
from jax.experimental import pallas as pl
from jax.experimental.pallas import tpu as pltpu
from jax.sharding import PartitionSpec as P

HD = 64
SEQ = 1024
STEP = 10
LANES = 128
QB = 256
BLOCKS = SEQ // QB
BIG = 1e30
LOG2E = 1.4426950408889634
LN2 = 0.6931471805599453
WINDOWS = (512, 640, 768, 1024)
BF = jnp.bfloat16
F32 = jnp.float32
I32 = jnp.int32


def nn(a, b):
    return jnp.dot(a, b, preferred_element_type=F32)


def nt(a, b):
    return lax.dot_general(a, b, (((1,), (1,)), ((), ())), preferred_element_type=F32)


def ds(start, size, step):
    return pl.ds(pl.multiple_of(start, step), size)


def shape(dims, dtype):
    return jax.ShapeDtypeStruct(dims, dtype)


def cost(flops, bytes_accessed, transcendentals=0):
    return pl.CostEstimate(
        flops=int(flops), bytes_accessed=int(bytes_accessed), transcendentals=int(transcendentals)
    )


SMEM = "smem"
HBM = "hbm"
OUT = "out"
SPACES = {SMEM: pltpu.SMEM, HBM: pltpu.HBM, OUT: pltpu.VMEM}
WHOLE = 63


def call(kernel, name, ins, outs, scratch, copies, estimate, mib=WHOLE):
    args = [
        pltpu.with_memory_space_constraint(array, pltpu.HBM) if space == HBM else array
        for space, array in ins
    ]
    return pl.pallas_call(
        kernel,
        out_shape=[
            pltpu.HBM(dims, dtype) if space == HBM else shape(dims, dtype)
            for space, dims, dtype in outs
        ],
        in_specs=[pl.BlockSpec(memory_space=SPACES[space]) for space, _ in ins],
        out_specs=[pl.BlockSpec(memory_space=SPACES[space]) for space, _, _ in outs],
        scratch_shapes=[pltpu.VMEM(dims, dtype) for dims, dtype in scratch]
        + [pltpu.SemaphoreType.DMA((max(copies, 1),))],
        compiler_params=pltpu.CompilerParams(vmem_limit_bytes=mib * 2**20),
        cost_estimate=estimate,
        name=name,
    )(*args)


class Copies:
    def __init__(self, sem):
        self.sem = sem
        self.used = 0
        self.pending = {}

    def start(self, name, *pairs):
        made = []
        for source, target in pairs:
            made.append(pltpu.make_async_copy(source, target, self.sem.at[self.used]))
            made[-1].start()
            self.used += 1
        self.pending[name] = made

    def wait(self, *names):
        for name in names:
            for copy in self.pending.pop(name):
                copy.wait()

    def finish(self):
        self.wait(*list(self.pending))


def lane_row():
    return lax.broadcasted_iota(I32, (1, LANES), 1)


def half_masks():
    low = jnp.where(lane_row() < HD, 1.0, 0.0)
    return (low.astype(BF), (1.0 - low).astype(BF))


def norm_rows(value):
    center = value - jnp.mean(value, axis=-1, keepdims=True)
    inv_std = lax.rsqrt(jnp.mean(center * center, axis=-1, keepdims=True) + 1e-05)
    return center * inv_std, inv_std


def norm_back(grad, normed, inv_std, gain):
    scaled = grad * gain
    mean_one = jnp.mean(scaled, axis=-1, keepdims=True)
    mean_two = jnp.mean(scaled * normed, axis=-1, keepdims=True)
    return inv_std * (scaled - mean_one - normed * mean_two)


def col_sum(value):
    return jnp.sum(value, axis=0, keepdims=True)


def sides(refs, target, index=None):
    size = target.shape[-1] // len(refs)
    picked = [ref if index is None else ref.at[index] for ref in refs]
    return [
        (ref, target.at[:, n * size : (n + 1) * size]) for n, ref in enumerate(picked)
    ]


def staged(count, *stages):
    for step in range(count + len(stages) - 1):
        for n, stage in enumerate(stages):
            if 0 <= step - n < count:
                stage(step - n)


def window_of(seg, real, i):
    begin = jnp.min(seg[2 * i : 2 * i + 1, :])
    end = jnp.max(seg[2 * i + 1 : 2 * i + 2, :])
    start = jnp.sum(jnp.where(seg < begin, 1, 0))
    stop = jnp.minimum(jnp.sum(jnp.where(seg <= end, 1, 0)), real)
    start = (start // LANES) * LANES
    need = stop - start
    kind = jnp.int32(0)
    size = jnp.int32(WINDOWS[0])
    for index, width in enumerate(WINDOWS[:-1]):
        kind = jnp.where(need > width, index + 1, kind)
        size = jnp.where(need > width, WINDOWS[index + 1], size)
    return jnp.minimum(start, SEQ - size), kind


def attention_kernel(
    core_ref, frames_ref, seg_ref, pad_ref, wm_ref, wo_ref, bm_ref, bo_ref,
    q_ref, k_ref, v_ref, augq_out, augk_out, mixed_ref, win_ref,
    x_s, w_s, q_s, k_s, v_s, vt_s, mt_s, lse_s, score_s, prob_s, mixed_s, augq_ref, augk_ref,
    small_s, seg_s, pad_s, sem,
):
    moves = Copies(sem)
    core = core_ref[0]
    lines = ds(core * (SEQ // LANES), SEQ // LANES, SEQ // LANES)
    moves.start("seg", (seg_ref.at[lines, :], seg_s), (pad_ref.at[lines, :], pad_s))
    moves.start("x", (frames_ref.at[ds(core * SEQ, SEQ, SEQ), :], x_s))
    moves.start("bias", *sides((bm_ref, bo_ref), small_s))
    moves.start(0, *sides((wm_ref, wo_ref), w_s.at[0], 0))
    lane = lane_row()
    moves.wait("seg")
    seg = seg_s[...]
    pad = pad_s[...]
    real = jnp.sum(pad)
    for i in range(BLOCKS):
        begin, kind = window_of(seg, real, i)
        win_ref[0, i] = begin
        win_ref[1, i] = kind
    for b in range(SEQ // LANES):
        rows = slice(b * LANES, (b + 1) * LANES)
        ids = jnp.broadcast_to(seg[b : b + 1, :].astype(F32), (LANES, LANES)).T
        shown = jnp.broadcast_to(pad[b : b + 1, :].astype(F32), (LANES, LANES)).T
        same = lane.astype(F32) == ids
        augk_ref[rows, :] = jnp.where(
            lane == 10, 1.0 - shown, jnp.where(same, 1.0, 0.0)
        ).astype(BF)
        off = jnp.where(same, 0.0, -BIG)
        augq_ref[rows, :] = jnp.where(
            lane < 10, off, jnp.where(lane == 10, -BIG, 0.0)
        ).astype(BF)
    moves.start("augk", (augk_ref, augk_out))
    moves.wait("bias", "x", 0)
    for j in (1, 2):
        moves.start(j, *sides((wm_ref, wo_ref), w_s.at[j], j))
    bias = [small_s[j : j + 1, :] for j in range(2)]
    q_s[...] = ((nn(x_s[...], w_s[0]) + bias[0]) * (HD ** (-0.5) * LOG2E)).astype(BF)
    moves.start("q", (q_s, q_ref))
    moves.wait(1)
    k_s[...] = nn(x_s[...], w_s[1]).astype(BF)
    moves.start("k", (k_s, k_ref))
    moves.wait(2)
    v_s[...] = (nn(x_s[...], w_s[2]) + bias[1]).astype(BF)
    moves.start("v", (v_s, v_ref))
    vt_s[...] = v_s[...].T
    lse_s[...] = jnp.zeros_like(lse_s)
    heads = q_s.shape[1] // HD
    masks = half_masks()

    def block(i, carry):
        rows = ds(i * QB, QB, QB)
        begin = win_ref[0, i]
        kind = win_ref[1, i]

        def run(width):
            span = ds(begin, width, LANES)
            ones = jnp.ones((16, width), BF)

            def score(h):
                tile = slice(h // 2 * LANES, (h // 2 + 1) * LANES)
                right = jnp.concatenate([q_s[rows, tile], augq_ref[rows, :]], axis=1)
                left = jnp.concatenate([k_s[span, tile] * masks[h % 2], augk_ref[span, :]], axis=1)
                score_s[h % 2, :width] = nt(left, right)

            def soften(h):
                top = jnp.max(score_s[h % 2, :width], axis=0, keepdims=True)
                prob_s[h % 2, :width] = jnp.exp2(score_s[h % 2, :width] - top).astype(BF)
                return top

            def mix(h, top):
                part = slice(h * HD, (h + 1) * HD)
                out = nn(jnp.concatenate([vt_s[part, span], ones], axis=0), prob_s[h % 2, :width])
                total = out[HD : HD + 1, :]
                mt_s[part, rows] = (out[:HD, :] * (1.0 / total)).astype(BF)
                lse = top + jnp.log2(total)
                for piece in range(3):
                    lse_s[16 * (piece + 1) + h : 16 * (piece + 1) + h + 1, rows] = lse

            tops = {}
            for step in range(heads + 2):
                if step < heads:
                    score(step)
                if step >= 2:
                    mix(step - 2, tops.pop(step - 2))
                if 1 <= step <= heads:
                    tops[step - 1] = soften(step - 1)

        for index, width in enumerate(WINDOWS):
            pl.when(kind == index)(functools.partial(run, width))
        mixed_s[rows, :] = mt_s[:, rows].T
        return carry

    lax.fori_loop(0, BLOCKS, block, 0)
    moves.start("mixed", (mixed_s, mixed_ref))
    lse = lse_s[...].T
    high = lse.astype(BF).astype(F32)
    mid = (lse - high).astype(BF).astype(F32)
    piece = jnp.where(lane < 32, high, jnp.where(lane < 48, mid, lse - high - mid))
    augq_ref[...] = (augq_ref[...].astype(F32) - piece).astype(BF)
    moves.start("augq", (augq_ref, augq_out))
    moves.finish()


def attention_forward(core, frames, seg, pad, att_m, att_o, bias_m, bias_o):
    width = frames.shape[1]
    wide = ((SEQ, width), BF)
    thin = ((SEQ, LANES), BF)
    line = ((SEQ // LANES, LANES), I32)
    return call(
        attention_kernel,
        "attention_forward",
        [(SMEM, core)]
        + [(HBM, a) for a in (frames, seg, pad, att_m, att_o, bias_m, bias_o)],
        [(HBM, *wide)] * 3 + [(HBM, *thin)] * 2 + [(HBM, *wide), (SMEM, (2, BLOCKS), I32)],
        [
            wide, ((3, width, width), BF), wide, wide, wide, ((width, SEQ), BF),
            ((width, SEQ), BF), ((LANES, SEQ), F32), ((2, SEQ, QB), F32), ((2, SEQ, QB), BF),
            wide, thin, thin, ((2, width), F32), line, line,
        ],
        17,
        cost(15e9, 20e6, 10e6),
    )


def gelu_pair(value):
    phi = 0.5 + 0.5 * lax.erf(value * 0.7071067811865476)
    low = value.astype(BF)
    density = jnp.exp2(low * low * BF(-0.5 * LOG2E)) * BF(0.3989422804014327)
    return (value * phi).astype(BF), phi.astype(BF) + low * density


def chunk_of(c, size):
    each = size // QB
    return c // each, ds(c % each * QB, QB, QB)


def forward_kernel(
    core_ref, frames_ref, cot_ref, mixed_ref, am_ref, ao_ref, fm_ref, fo_ref, hm_ref, ho_ref,
    augk_out, vec_out,
    n1_ref, inv_out, low_ref, out_ref, g2_ref, glow_ref, slope_ref, dm_ref, do_ref, sum_ref,
    x_s, mixed_s, wo_s, w1_s, w2_s, cot_s, n1_s, inv_ref, low_s, g2_s, glow_s, slope_s, act_s,
    glt_s, stage_s, unit_s, ffn_s, bias_s, augk_ref, vec_ref, sem,
):
    units = fm_ref.shape[2]
    moves = Copies(sem)
    own = ds(core_ref[0] * SEQ, SEQ, SEQ)
    moves.start("wo", *sides((am_ref, ao_ref), wo_s, 3))
    moves.start("in", (vec_out, vec_ref), (mixed_ref, mixed_s), (frames_ref.at[own, :], x_s))
    moves.start("bias", *sides((hm_ref, ho_ref), bias_s))
    moves.wait("wo", "in")
    moves.start("w1", *sides((fm_ref, fo_ref), w1_s, 0))
    sum_ref[...] = jnp.zeros_like(sum_ref)

    def project(r):
        rows = slice(r * QB, (r + 1) * QB)
        ffn_s[r % 2] = nt(mixed_s[rows, :], wo_s[...])

    def first_rows(r):
        rows = slice(r * QB, (r + 1) * QB)
        first = x_s[rows, :].astype(F32) + ffn_s[r % 2] + vec_ref[0:1, :]
        normed, inv_std = norm_rows(first)
        n1_s[rows, :] = normed
        inv_ref[rows, :] = jnp.broadcast_to(inv_std, (QB, LANES))
        low_s[rows, :] = (normed * vec_ref[1:2, :] + vec_ref[2:3, :]).astype(BF)

    staged(BLOCKS, project, first_rows)
    moves.wait("bias", "w1")
    moves.start("first", (n1_s, n1_ref), (inv_ref, inv_out), (low_s, low_ref))
    moves.start("cot", (cot_ref.at[own, :], cot_s), (augk_out, augk_ref))
    moves.start("w2", *sides((fm_ref, fo_ref), w2_s, 1))
    each = units // QB

    def up(c):
        unit_s[c % 2] = nn(low_s[...], w1_s[:, c * QB : (c + 1) * QB])

    def bend(c):
        spot = slice(c * QB, (c + 1) * QB)
        act, slope = gelu_pair(unit_s[c % 2] + bias_s[0:1, spot])
        act_s[:, c * QB : (c + 1) * QB] = act
        slope_s[:, c * QB : (c + 1) * QB] = slope

    staged(2 * each, up, bend)
    moves.start("slope", (slope_s, slope_ref))
    moves.wait("cot", "w2")

    def contract(r):
        rows = slice(r * QB, (r + 1) * QB)
        ffn_s[r % 2] = nt(act_s[rows, :], w2_s[...])

    def second(r):
        rows = slice(r * QB, (r + 1) * QB)
        first_norm = n1_s[rows, :] * vec_ref[1:2, :] + vec_ref[2:3, :]
        n2, inv_std = norm_rows(first_norm + ffn_s[r % 2] + vec_ref[3:4, :])
        valid = 1.0 - augk_ref[rows, 10:11].astype(F32)
        grad = cot_s[rows, :].astype(F32) * valid
        cot_s[rows, :] = (n2 * vec_ref[4:5, :] + vec_ref[5:6, :]).astype(BF)
        back = norm_back(grad, n2, inv_std, vec_ref[4:5, :])
        g2_s[rows, :] = back
        glow_s[rows, :] = back.astype(BF)
        sum_ref[3:4, :] += col_sum(back)
        sum_ref[4:5, :] += col_sum(grad * n2)
        sum_ref[5:6, :] += col_sum(grad)

    staged(BLOCKS, contract, second)
    moves.start("second", (cot_s, out_ref), (g2_s, g2_ref), (glow_s, glow_ref))
    glt_s[...] = glow_s[...].T
    size = stage_s.shape[2]
    spots = [(side, part) for side in (1, 0) for part in range(3)]
    for n, (side, part) in enumerate(spots):
        if n >= 2:
            moves.wait(n - 2)
        for c in range(size // QB):
            at = side * units + part * size + c * QB
            grad = nn(glt_s[...], act_s[:, at : at + QB])
            stage_s[n % 2, :, c * QB : (c + 1) * QB] = grad.astype(BF)
        moves.start(n, (stage_s.at[n % 2], (dm_ref, do_ref)[side].at[part]))
    moves.finish()


def ffn_forward(
    core, frames, cot, mixed, att_m, att_o, ffw_m, ffw_o, hid_m, hid_o, augk, vectors
):
    width = frames.shape[1]
    units = ffw_m.shape[2]
    wide = ((SEQ, width), BF)
    full = ((SEQ, width), F32)
    thin = ((SEQ, LANES), F32)
    inner = ((width, 2 * units), BF)
    outer = ((SEQ, 2 * units), BF)
    grads = ((3, width, units // 3), BF)
    ins = (frames, cot, mixed, att_m, att_o, ffw_m, ffw_o, hid_m, hid_o, augk, vectors)
    return call(
        forward_kernel,
        "ffn_forward",
        [(SMEM, core)] + [(HBM, a) for a in ins],
        [(HBM, *out) for out in (full, thin, wide, wide, full, wide, outer, grads, grads)]
        + [(OUT, (8, width), F32)],
        [
            wide, wide, ((width, width), BF), inner, inner, wide, full, thin, wide, full, wide,
            outer, outer, ((width, SEQ), BF), ((2, width, units // 3), BF), ((2, SEQ, QB), F32),
            ((2, QB, width), F32), ((1, 2 * units), F32), ((SEQ, LANES), BF),
            (vectors.shape, F32),
        ],
        26,
        cost(15.7e9, 40e6, 6e6),
    )


def hidden_kernel(
    glow_ref, slope_ref, low_ref, fm_ref, fo_ref,
    gup_ref, um_ref, uo_ref, hm_ref, ho_ref,
    glow_s, slope_s, low_s, w2_s, lowt_s, um_s, uo_s, unit_s, sem,
):
    units = fm_ref.shape[2]
    half = [slice(side * units, (side + 1) * units) for side in range(2)]
    moves = Copies(sem)

    def weight(side):
        return (fm_ref, fo_ref)[side].at[1], w2_s.at[:, half[side]]

    def slope(side):
        return slope_ref.at[:, half[side]], slope_s.at[:, half[side]]

    moves.start("first", (glow_ref, glow_s), weight(1))
    moves.wait("first")
    moves.start("low", (low_ref, low_s), slope(1))
    gup_s = slope_s
    each = units // QB
    targets = ((um_s, um_ref, hm_ref), (uo_s, uo_ref, ho_ref))
    order = [(side, c) for side in (1, 0) for c in range(each)]

    def place(n):
        side, c = order[n]
        at = side * units + c * QB
        return side, c, slice(at, at + QB), slice(c * QB, (c + 1) * QB)

    def pull(n):
        side, c, there, here = place(n)
        if n == each:
            moves.wait("rest")
        unit_s[n % 2] = nn(glow_s[...], w2_s[:, there])
        if n == 0:
            moves.wait("low")
            moves.start("rest", weight(0), slope(0))
            lowt_s[...] = low_s[...].T

    def bend(n):
        side, c, there, here = place(n)
        grad = (unit_s[n % 2] * slope_s[:, there].astype(F32)).astype(BF)
        gup_s[:, there] = grad
        targets[side][2][0:1, here] = col_sum(grad.astype(F32))

    def push(n):
        side, c, there, here = place(n)
        target, result, bias = targets[side]
        part, spot = divmod(c * QB, target.shape[2])
        target[part, :, spot : spot + QB] = nn(lowt_s[...], gup_s[:, there]).astype(BF)
        if c == each - 1:
            moves.start(
                side,
                (target, result),
                (gup_s.at[:, half[side]], gup_ref.at[:, half[side]]),
            )

    staged(2 * each, pull, bend, push)
    moves.finish()


def hidden_backward(glow, slope, low, ffw_m, ffw_o):
    width = low.shape[1]
    units = ffw_m.shape[2]
    wide = ((SEQ, width), BF)
    outer = ((SEQ, 2 * units), BF)
    grads = ((3, width, units // 3), BF)
    return call(
        hidden_kernel,
        "hidden_backward",
        [(HBM, a) for a in (glow, slope, low, ffw_m, ffw_o)],
        [
            (HBM, *outer), (HBM, *grads), (HBM, *grads),
            (OUT, (1, units), F32), (OUT, (1, units), F32),
        ],
        [
            wide, outer, wide, ((width, 2 * units), BF), ((width, SEQ), BF), grads, grads,
            ((2, SEQ, QB), F32),
        ],
        10,
        cost(9.7e9, 30e6),
    )


def norm_kernel(
    gup_ref, g2_ref, n1_ref, inv_out, mixed_ref, fm_ref, fo_ref, am_ref, ao_ref, vec_out,
    g1_ref, om_ref, oo_ref, gm_ref, augd_out, sum_ref,
    gup_s, g2_s, n1_s, inv_ref, mixed_s, w1_s, wo_s, vec_ref,
    glow_s, glt_s, gm_s, augd_ref, om_s, oo_s, gfn_s, sem,
):
    moves = Copies(sem)
    g1_s = g2_s
    moves.start("w1", *sides((fm_ref, fo_ref), w1_s, 0))

    def fetch(r):
        rows = slice(r * QB, (r + 1) * QB)
        moves.start(("gup", r), (gup_ref.at[rows, :], gup_s.at[rows, :]))
        moves.start(
            ("first", r),
            (g2_ref.at[rows, :], g2_s.at[rows, :]),
            (n1_ref.at[rows, :], n1_s.at[rows, :]),
        )

    moves.start("vec", (vec_out, vec_ref), (inv_out, inv_ref))
    fetch(0)
    sum_ref[...] = jnp.zeros_like(sum_ref)
    moves.wait("w1", "vec")
    fetch(1)

    def pull(r):
        rows = slice(r * QB, (r + 1) * QB)
        moves.wait(("gup", r))
        if 0 < r < BLOCKS - 1:
            fetch(r + 1)
        gfn_s[r % 2] = nt(gup_s[rows, :], w1_s[...])
        if r == BLOCKS - 1:
            moves.start("wo", *sides((am_ref, ao_ref), wo_s, 3))
            moves.start("mixed", (mixed_ref, mixed_s))

    def first_rows(r):
        rows = slice(r * QB, (r + 1) * QB)
        moves.wait(("first", r))
        grad = gfn_s[r % 2] + g2_s[rows, :]
        n1 = n1_s[rows, :]
        back = norm_back(grad, n1, inv_ref[rows, 0:1], vec_ref[1:2, :])
        g1_s[rows, :] = back
        glow_s[rows, :] = back.astype(BF)
        sum_ref[0:1, :] += col_sum(back)
        sum_ref[1:2, :] += col_sum(grad * n1)
        sum_ref[2:3, :] += col_sum(grad)

    staged(BLOCKS, pull, first_rows)
    moves.start("g1", (g1_s, g1_ref))
    moves.wait("wo", "mixed")
    lane = lane_row()
    width = wo_s.shape[0]
    head = lax.broadcasted_iota(I32, (width, LANES), 0) // HD
    spot = lax.broadcasted_iota(I32, (width, LANES), 1)
    pick = jnp.where((spot == head + 16) | (spot == head + 32), 1.0, 0.0).astype(BF)
    for r in range(BLOCKS):
        rows = slice(r * QB, (r + 1) * QB)
        gm = nn(glow_s[rows, :], wo_s[...]).astype(BF)
        gm_s[rows, :] = gm
        both = gm.astype(F32) * mixed_s[rows, :].astype(F32)
        high = both.astype(BF)
        dots = nn(high, pick) + nn((both - high.astype(F32)).astype(BF), pick)
        dot_high = dots.astype(BF).astype(F32)
        augd_ref[rows, :] = (-jnp.where(lane < 32, dot_high, dots - dot_high)).astype(BF)
    moves.start("gm", (gm_s, gm_ref), (augd_ref, augd_out))
    glt_s[...] = glow_s[...].T
    size = om_s.shape[2]
    for side, target, result in ((1, oo_s, oo_ref), (0, om_s, om_ref)):
        cols = slice(side * 3 * size, (side + 1) * 3 * size)
        product = nn(glt_s[...], mixed_s[:, cols]).astype(BF)
        for part in range(3):
            target[part] = product[:, part * size : (part + 1) * size]
        moves.start(("o", side), (target, result))
    moves.finish()


def norm_backward(gup, g2, n1, inv, mixed, ffw_m, ffw_o, att_m, att_o, vectors):
    width = n1.shape[1]
    units = ffw_m.shape[2]
    cols = att_m.shape[2]
    wide = ((SEQ, width), BF)
    full = ((SEQ, width), F32)
    thin = ((SEQ, LANES), BF)
    grads = ((3, width, cols // 3), BF)
    ins = (gup, g2, n1, inv, mixed, ffw_m, ffw_o, att_m, att_o, vectors)
    return call(
        norm_kernel,
        "norm_backward",
        [(HBM, a) for a in ins],
        [(HBM, *out) for out in (full, grads, grads, wide, thin)] + [(OUT, (8, width), F32)],
        [
            ((SEQ, 2 * units), BF), full, full, ((SEQ, LANES), F32), wide,
            ((width, 2 * units), BF), ((width, width), BF), (vectors.shape, F32),
            wide, ((width, SEQ), BF), wide, thin, grads, grads, ((2, QB, width), F32),
        ],
        27,
        cost(7.5e9, 30e6),
    )


def heads_kernel(
    side,
    win_ref, core_ref, q_ref, k_ref, v_ref, gm_ref, augq_out, augd_out, augk_out, frames_ref,
    dq_ref, dk_ref, dv_ref, grad_ref, bias_ref,
    q_s, k_s, v_s, gm_s, augq_ref, augd_ref, augk_ref, x_s,
    kt_s, dqt_s, dk_s, dv_s, xt_s, score_s, slope_s, prob_s, back_s, outs_s, grad_s, sem,
):
    cols = dk_s.shape[1]
    heads = cols // HD
    moves = Copies(sem)
    own = slice(side * cols, (side + 1) * cols)
    moves.start(
        "in",
        *[
            (ref.at[:, own], to)
            for ref, to in ((k_ref, k_s), (q_ref, q_s), (v_ref, v_s), (gm_ref, gm_s))
        ],
        (augq_out, augq_ref), (augd_out, augd_ref), (augk_out, augk_ref),
    )
    dk_s[...] = jnp.zeros_like(dk_s)
    dv_s[...] = jnp.zeros_like(dv_s)
    moves.wait("in")
    moves.start("x", (frames_ref.at[ds(core_ref[0] * SEQ, SEQ, SEQ), :], x_s))
    kt_s[...] = k_s[...].T
    masks = half_masks()
    lane = lane_row()

    def block(i, carry):
        rows = ds(i * QB, QB, QB)
        begin = win_ref[0, i]
        kind = win_ref[1, i]

        def run(width):
            span = ds(begin, width, LANES)

            def scores(h):
                tile = slice(h // 2 * LANES, (h // 2 + 1) * LANES)
                at = side * heads + h
                ones = jnp.where((lane == at + 16) | (lane == at + 32), 1.0, 0.0)
                more = jnp.where(lane == at + 48, 1.0, ones).astype(BF)
                ones = ones.astype(BF)
                mask = masks[h % 2]
                score_s[h % 2, :width] = nt(
                    jnp.concatenate([k_s[span, tile] * mask, augk_ref[span, :] + more], axis=1),
                    jnp.concatenate([q_s[rows, tile], augq_ref[rows, :]], axis=1),
                )
                slope_s[h % 2, :width] = nt(
                    jnp.concatenate(
                        [v_s[span, tile] * mask, jnp.broadcast_to(ones, (width, LANES))], axis=1
                    ),
                    jnp.concatenate([gm_s[rows, tile], augd_ref[rows, :]], axis=1),
                )

            def soften(h):
                probs = jnp.exp2(score_s[h % 2, :width])
                prob_s[h % 2, :width] = probs.astype(BF)
                back_s[h % 2, :width] = (probs * slope_s[h % 2, :width]).astype(BF)

            def collect(h):
                tile = slice(h // 2 * LANES, (h // 2 + 1) * LANES)
                mask = masks[h % 2]
                dv_s[span, tile] += nn(prob_s[h % 2, :width], gm_s[rows, tile] * mask)
                dk_s[span, tile] += nn(back_s[h % 2, :width], q_s[rows, tile] * mask)
                here = slice(h * HD, (h + 1) * HD)
                dqt_s[here, rows] = nn(kt_s[here, span], back_s[h % 2, :width])

            for step in range(heads + 2):
                if step < heads:
                    scores(step)
                if step >= 2:
                    collect(step - 2)
                if 1 <= step <= heads:
                    soften(step - 1)

        for index, width in enumerate(WINDOWS):
            pl.when(kind == index)(functools.partial(run, width))
        return carry

    lax.fori_loop(0, BLOCKS, block, 0)
    bias_ref[...] = jnp.zeros_like(bias_ref)
    bias_ref[...] = jnp.zeros_like(bias_ref)
    outs_s[0] = (dqt_s[...] * HD ** (-0.5)).T.astype(BF)
    outs_s[1] = (dk_s[...] * LN2).astype(BF)
    outs_s[2] = dv_s[...].astype(BF)
    moves.start("out", *[(outs_s.at[j], ref) for j, ref in enumerate((dq_ref, dk_ref, dv_ref))])
    bias_ref[0:1, :] = col_sum(outs_s[0].astype(F32))
    bias_ref[1:2, :] = col_sum(outs_s[2].astype(F32))
    moves.wait("x")
    xt_s[...] = x_s[...].T
    for j in range(3):
        grad_s[j] = nn(xt_s[...], outs_s[j]).astype(BF)
        moves.start(j, (grad_s.at[j], grad_ref.at[j]))
    moves.finish()


def heads_backward(side, cols, win, core, q, k, v, gm, augq, augd, augk, frames):
    width = frames.shape[1]
    part = ((SEQ, cols), BF)
    thin = ((SEQ, LANES), BF)
    sums = ((SEQ, cols), F32)
    grads = ((3, width, cols), BF)
    return call(
        functools.partial(heads_kernel, side),
        "heads_backward",
        [(SMEM, win), (SMEM, core)]
        + [(HBM, a) for a in (q, k, v, gm, augq, augd, augk, frames)],
        [(HBM, *out) for out in (part, part, part, grads)] + [(OUT, (8, cols), F32)],
        [
            part, part, part, part, thin, thin, thin, ((SEQ, width), BF),
            ((cols, SEQ), BF), ((cols, SEQ), F32), sums, sums, ((width, SEQ), BF),
            ((2, SEQ, QB), F32), ((2, SEQ, QB), F32), ((2, SEQ, QB), BF), ((2, SEQ, QB), BF),
            ((3, SEQ, cols), BF), grads,
        ],
        14,
        cost(12e9, 15e6, 5e6),
    )


def input_kernel(
    qm_ref, km_ref, vm_ref, qo_ref, ko_ref, vo_ref, g1_ref, wm_ref, wo_ref, out_ref,
    w_s, left_s, g1_s, out_s, sem,
):
    cols = wm_ref.shape[2]
    moves = Copies(sem)
    for j in range(3):
        at = slice(2 * j * cols, 2 * (j + 1) * cols)
        moves.start(("w", j), *sides((wm_ref, wo_ref), w_s.at[:, at], j))
    refs = (qm_ref, qo_ref, km_ref, ko_ref, vm_ref, vo_ref)

    def fetch(r):
        rows = slice(r * QB, (r + 1) * QB)
        moves.start(
            r,
            (g1_ref.at[rows, :], g1_s.at[rows, :]),
            *[
                (ref.at[rows, :], left_s.at[rows, n * cols : (n + 1) * cols])
                for n, ref in enumerate(refs)
            ],
        )

    fetch(0)
    moves.wait(*[("w", j) for j in range(3)])
    fetch(1)
    for r in range(BLOCKS):
        rows = slice(r * QB, (r + 1) * QB)
        moves.wait(r)
        if 0 < r < BLOCKS - 1:
            fetch(r + 1)
        out_s[rows, :] = (nt(left_s[rows, :], w_s[...]) + g1_s[rows, :]).astype(BF)
        moves.start(("out", r), (out_s.at[rows, :], out_ref.at[rows, :]))
    moves.finish()


def input_gradient(mine, other, g1, att_m, att_o):
    width = g1.shape[1]
    return call(
        input_kernel,
        "input_gradient",
        [(HBM, a) for a in (*mine, *other, g1, att_m, att_o)],
        [(HBM, (SEQ, width), BF)],
        [
            ((width, 3 * width), BF), ((SEQ, 3 * width), BF), ((SEQ, width), F32),
            ((SEQ, width), BF),
        ],
        6 + 8 * BLOCKS,
        cost(3.6e9, 15e6),
    )[0]


def swap_cores(value):
    return lax.ppermute(value, "tensor", [(0, 1), (1, 0)])


def swap_bit(value, bit, count):
    return lax.ppermute(value, "dp", [(i, i ^ (1 << bit)) for i in range(count)])


class Reduction:
    def __init__(self, count):
        self.count = count
        self.bits = count.bit_length() - 1
        self.step = 0
        self.regions = []
        turn = min(self.bits, 3)
        self.orders = [
            [(n + s) % turn for s in range(turn)] + list(range(turn, self.bits)) for n in range(3)
        ]
        self.sources = [[] for _ in range(3)]

    @property
    def columns(self):
        return sum(width for _, width in self.regions)

    def add(self, mine, other):
        self.rows = mine.shape[1] // self.count
        width = mine.shape[2]
        view = (3,) + (2,) * self.bits + (self.rows, width)
        every = list(range(self.bits - 1, -1, -1))
        at = self.columns
        for value in (mine.reshape(view), swap_cores(other).reshape(view)):
            for part in range(3):
                self.sources[part].append((value, part, every, at, width))
        self.regions.append((at, width))

    def left(self, part, step):
        gone = self.orders[part][:step]
        return [b for b in range(self.bits - 1, -1, -1) if b not in gone]

    def jobs(self, final):
        step = self.bits if final else self.step + 1
        sent = [None if final else order[self.step] for order in self.orders]
        joined = len(set(sent)) == 1
        outs = []
        jobs = []
        for part in range(3):
            bits = self.left(part, step)
            dims = (2,) * len(bits) + (self.rows, self.columns)
            if joined:
                if part == 0:
                    outs.append(((3,) + dims, F32 if final else BF))
                jobs.append((0, part, bits, sent[part], self.sources[part], self.regions))
            else:
                outs.append((dims, BF))
                jobs.append((part, None, bits, sent[part], self.sources[part], self.regions))
        return outs, jobs

    def launch(self, sends):
        turn = [order[self.step] for order in self.orders]
        if len(sends) == 1:
            got = swap_bit(sends[0], turn[0], self.count)
            moved = [(got, n) for n in range(3)]
        else:
            moved = [(swap_bit(s, b, self.count), None) for s, b in zip(sends, turn)]
        self.step += 1
        for part, (value, lead) in enumerate(moved):
            bits = self.left(part, self.step)
            self.sources[part].append((value, lead, bits, 0, self.columns))


def fold_kernel(jobs, inputs, outputs, final, place_ref, *refs):
    ins, refs = refs[:inputs], refs[inputs:]
    results, refs = refs[:outputs], refs[outputs:]
    if final:
        squares_ref, refs = refs[0], refs[1:]
    scratch, outs = refs[: -1 - outputs], refs[-1 - outputs : -1]
    moves = Copies(refs[-1])
    spot = 0
    for output, lead, bits, sent, sources, regions in jobs:
        for which, part, own_bits, at, width in sources:
            index = [] if part is None else [part]
            for bit in own_bits:
                if bit in bits:
                    index.append(slice(None))
                else:
                    index.append(1 - place_ref[bit] if bit == sent else place_ref[bit])
            moves.start(spot, (ins[which].at[tuple(index)], scratch[spot]))
            spot += 1
    squares = jnp.float32(0.0)
    spot = 0
    for number, (output, lead, bits, sent, sources, regions) in enumerate(jobs):
        target = outs[output] if lead is None else outs[output].at[lead]
        for n in range(len(sources)):
            moves.wait(spot + n)
        for at, width in regions:
            total = None
            for n, (which, part, own_bits, first, size) in enumerate(sources):
                if first <= at < first + size:
                    value = scratch[spot + n][..., at - first : at - first + width].astype(F32)
                    total = value if total is None else total + value
            target[..., at : at + width] = total.astype(target.dtype)
            if final:
                squares = squares + jnp.sum(total * total)
        spot += len(sources)
        if output not in [job[0] for job in jobs[number + 1 :]]:
            moves.start(("out", output), (outs[output], results[output]))
    moves.finish()
    if final:
        squares_ref[0, 0] = squares


def fold(place, reductions, final=False):
    arrays = []
    outs = []
    jobs = []
    counts = []
    for reduction in reductions:
        shapes, todo = reduction.jobs(final)
        for output, lead, bits, sent, sources, regions in todo:
            listed = []
            for array, part, own_bits, at, width in sources:
                known = [n for n, a in enumerate(arrays) if a is array]
                if not known:
                    arrays.append(array)
                listed.append((known[0] if known else len(arrays) - 1, part, own_bits, at, width))
            jobs.append((len(outs) + output, lead, bits, sent, listed, regions))
        outs += shapes
        counts.append(len(shapes))
    scratch = []
    for output, lead, bits, sent, sources, regions in jobs:
        for which, part, own_bits, at, width in sources:
            rows = arrays[which].shape[-2]
            scratch.append(((2,) * len(bits) + (rows, width), BF))
    size = sum(functools.reduce(lambda a, b: a * b, dims) for dims, _ in scratch)
    res = call(
        functools.partial(fold_kernel, jobs, len(arrays), len(outs), final),
        "fold",
        [(SMEM, place)] + [(HBM, a) for a in arrays],
        [(HBM, *out) for out in outs] + ([(SMEM, (1, 1), F32)] if final else []),
        scratch + [out for out in outs],
        len(scratch) + len(outs),
        cost(2 * size, 6 * size),
    )
    grouped = []
    at = 0
    for n in counts:
        grouped.append(res[at : at + n])
        at += n
    return grouped + ([res[-1]] if final else [])


def advance(place, reductions, *held):
    sends = fold(place, reductions)
    sends, held = lax.optimization_barrier((sends, held))
    for reduction, send in zip(reductions, sends):
        reduction.launch(send)
    return held


def update_kernel(
    factor_ref, down_ref, up_ref, qkv_ref, aw, am, av, fw, fm, fv, *refs
):
    factor = factor_ref[0, 0]
    small, outs = refs[:12], refs[12:]

    def adam(grad, weight, first, second, results, index, rate, decay):
        clipped = grad * factor
        first_new = 0.9 * first[index] + 0.1 * clipped
        second_new = 0.999 * second[index] + 0.001 * clipped * clipped
        mean_hat = first_new / (1.0 - 0.9**STEP)
        var_hat = second_new / (1.0 - 0.999**STEP)
        old = weight[index].astype(F32)
        results[0][index] = first_new
        results[1][index] = second_new
        results[2][index] = old - rate * (mean_hat / (jnp.sqrt(var_hat) + 1e-08) + decay * old)

    every = slice(None)
    each = down_ref.shape[2]
    rest = up_ref.shape[2] - each
    for j in range(3):
        adam(qkv_ref[j], aw, am, av, outs[0:3], (j,), 0.05, 0.01)
        cols = slice(j * rest, (j + 1) * rest)
        adam(up_ref[j, :, each:], aw, am, av, outs[0:3], (3, every, cols), 0.05, 0.01)
        cols = slice(j * each, (j + 1) * each)
        adam(up_ref[j, :, :each], fw, fm, fv, outs[3:6], (0, every, cols), 0.05, 0.01)
        adam(down_ref[j], fw, fm, fv, outs[3:6], (1, every, cols), 0.05, 0.01)
    for n in range(3):
        grad, weight, first, second = small[4 * n : 4 * n + 4]
        results = outs[6 + 3 * n : 9 + 3 * n]
        adam(grad[...], weight, first, second, results, (every, every), 0.5, 0.0)


def update(factor, down, up, qkv, attention, feedforward, small):
    arrays = [down, up, qkv, *attention, *feedforward]
    outs = [attention[1].shape] * 3 + [feedforward[1].shape] * 3
    for group in small:
        arrays += group
        outs += [group[0].shape] * 3
    return call(
        update_kernel,
        "update",
        [(SMEM, factor)] + [(OUT, a) for a in arrays],
        [(OUT, dims, F32) for dims in outs],
        [],
        0,
        cost(5e6, 6e6),
        mib=16,
    )


def local(
    frames,
    cotangent,
    segment_ids,
    pad_mask,
    attention_weight,
    feedforward_weight,
    head_bias,
    hidden_bias,
    norm_vectors,
    attention_first,
    attention_second,
    feedforward_first,
    feedforward_second,
    head_first,
    head_second,
    hidden_first,
    hidden_second,
    vector_first,
    vector_second,
):
    width = frames.shape[1]
    cols = attention_weight.shape[2]
    units = feedforward_weight.shape[2]
    count = lax.axis_size("dp")
    bits = count.bit_length() - 1
    rows = width // count
    core = lax.axis_index("tensor")
    dp_index = lax.axis_index("dp")
    core_ref = core.reshape(1).astype(I32)
    place = jnp.stack([(dp_index >> b) & 1 for b in range(bits)]).astype(I32)

    att_m, ffw_m, hid_m = attention_weight, feedforward_weight, hidden_bias
    head_m = head_bias.reshape(2, cols)
    att_o = swap_cores(att_m)
    head_o = swap_cores(head_m)
    hid_o = swap_cores(hid_m)
    ffw_late, att_o = lax.optimization_barrier((ffw_m, att_o))
    ffw_o = swap_cores(ffw_late)
    lines = (frames.shape[0] // LANES, LANES)

    q, k, v, augq, augk, mixed, win = attention_forward(
        core_ref, frames, segment_ids.reshape(lines), pad_mask.reshape(lines), att_m, att_o,
        head_m, head_o,
    )
    n1, inv, low, out_row, g2, glow, slope, down_m, down_o, sums_two = ffn_forward(
        core_ref, frames, cotangent, mixed, att_m, att_o, ffw_m, ffw_o, hid_m, hid_o, augk,
        norm_vectors,
    )
    down = Reduction(count)
    down.add(down_m, down_o)
    gup, up_m, up_o, hidden_m, hidden_o = hidden_backward(glow, slope, low, ffw_m, ffw_o)
    up = Reduction(count)
    up.add(up_m, up_o)
    (gup,) = advance(place, [down], gup)
    g1, om, oo, gm, augd, sums_one = norm_backward(
        gup, g2, n1, inv, mixed, ffw_m, ffw_o, att_m, att_o, norm_vectors
    )
    up.add(om, oo)
    (gm,) = advance(place, [down, up], gm)

    def back(side, gm):
        return heads_backward(
            side, cols, win, core_ref, q, k, v, gm, augq, augd, augk, frames
        )

    *other, other_grad, other_bias = back(1, gm)
    gm, other_grad = advance(place, [down, up], gm, other_grad)
    *mine, mine_grad, mine_bias = back(0, gm)
    qkv = Reduction(count)
    qkv.add(mine_grad, other_grad)

    side_sums = jnp.concatenate(
        [hidden_m.reshape(-1), mine_bias[:2].reshape(-1)]
    ) + swap_cores(jnp.concatenate([hidden_o.reshape(-1), other_bias[:2].reshape(-1)]))
    vector_sums = jnp.concatenate([sums_one[0:3], sums_two[3:6]], axis=0)
    vector_sums = vector_sums + swap_cores(vector_sums)
    small = jnp.concatenate([side_sums, vector_sums.reshape(-1)])
    for bit in range(bits):
        active = [r for r in (qkv, up, down) if r.step < bits]
        advance(place, active)
        small = small + swap_bit(small, bit, count)
    hidden_sum = small[:units]
    head_sum = small[units : units + 2 * cols]
    vector_sum = small[units + 2 * cols :]
    grad_row = input_gradient(mine, other, g1, att_m, att_o)

    (down_sum,), (up_sum,), early = fold(place, [down, up], final=True)
    (qkv_sum,), late = fold(place, [qkv], final=True)
    squares = (jnp.sum(hidden_sum * hidden_sum) + jnp.sum(head_sum * head_sum)) / count
    squares = squares + jnp.sum(vector_sum * vector_sum) / (2 * count)
    squares = squares + early + late
    squares = squares + swap_cores(squares)
    for bit in range(bits):
        squares = squares + swap_bit(squares, bit, count)
    gradient_norm = jnp.sqrt(squares)
    factor = jnp.minimum(1.0, 1.0 / (gradient_norm + 1e-06))

    def own(value, size, axis):
        return lax.dynamic_slice_in_dim(value, dp_index * size, size, axis)

    def flat(value):
        return value.reshape(-1, value.shape[-1])

    new = update(
        factor, down_sum, up_sum, qkv_sum,
        (own(att_m, rows, 1), attention_first, attention_second),
        (own(ffw_m, rows, 1), feedforward_first, feedforward_second),
        (
            (
                own(head_sum.reshape(2, cols), cols // count, 1), own(head_m, cols // count, 1),
                flat(head_first), flat(head_second),
            ),
            (
                own(hidden_sum.reshape(1, units), units // count, 1),
                own(hidden_bias, units // count, 1), hidden_first, hidden_second,
            ),
            (
                own(vector_sum.reshape(6, width), rows, 1), own(norm_vectors, rows, 1),
                vector_first, vector_second,
            ),
        ),
    )

    def both_rows(row):
        partner = swap_cores(row)
        lower = jnp.where(core == 0, row, partner)
        upper = jnp.where(core == 0, partner, row)
        return jnp.concatenate([lower, upper], axis=0)

    return (
        both_rows(out_row),
        both_rows(grad_row).astype(F32),
        gradient_norm.reshape(()),
        *new[:6],
        *[value.reshape(head_first.shape) for value in new[6:9]],
        *new[9:],
    )


def solution(mesh):
    weight_spec = P(None, None, "tensor")
    shard = P(None, "dp", "tensor")
    head = P(None, "tensor", "dp")
    hidden = P("tensor", "dp")
    vector = P(None, "dp")
    row = P("dp", None)
    return jax.shard_map(
        local,
        mesh=mesh,
        in_specs=(
            row, row, P("dp"), P("dp"),
            weight_spec, weight_spec,
            P(None, "tensor", None), P("tensor", None), P(),
            shard, shard, shard, shard,
            head, head, hidden, hidden, vector, vector,
        ),
        out_specs=(
            row, row, P(),
            shard, shard, shard, shard, shard, shard,
            head, head, head, hidden, hidden, hidden, vector, vector, vector,
        ),
        check_vma=False,
    )
```

time: 1160 us -> 320 us (0.28)
  waiting for transfers between devices: 622 us -> 45.9 us
  matrix products: 224 us -> 0 us
  Pallas kernels: 0 us -> 169 us
  other arithmetic: 144 us -> 17.2 us
  blocking collectives: 81.6 us -> 0 us
  starting transfers between devices: 1.45 us -> 53.3 us
  local copies, waits for them, and re-layouts: 54.1 us -> 20.4 us
  between operations: 21.9 us -> 9.13 us
    reduce_scatter x2 -> x0, waiting for transfers between devices: 314 us -> none  [the longest x1 174 us: local(): lax.psum_scatter(totals[1], 'dp', scatter_dimension=1, tiled=True)]
    dot_general x48 -> x0, matrix products: 224 us -> none  [the longest x2 41 us: micro_pass(): jnp.dot(first_low, ffw_w[0], preferred_element_type=jnp.float32)]
    unnamed x6 -> x0, waiting for transfers between devices: 200 us -> none
    pallas_call x0 -> x17, Pallas kernels: none -> 169 us  [call(): pl.pallas_call(kernel, out_shape=[pltpu.HBM(dims, dtype) if space == HBM...]
    psum x8 -> x0, waiting for transfers between devices: 108 us -> none  [the longest x2 42.2 us: micro_pass(): attn_total = lax.psum(partial_value, 'tensor').astype(jnp.float32)]
    ppermute x0 -> x51, starting transfers between devices: none -> 53.3 us  [the longest x38 49.4 us: swap_bit(): return lax.ppermute(value, 'dp', [(i, i ^ 1 << bit) for i in range(count)])]
    reduce_sum x25 -> x0, other arithmetic: 53.2 us -> none  [the longest x4 12.3 us: norm_back(): return (back, jnp.sum(grad * normed, axis=0), jnp.sum(grad, axis=0))]
    ppermute x0 -> x51, waiting for transfers between devices: none -> 45.9 us  [the longest x38 34.7 us: swap_bit(): return lax.ppermute(value, 'dp', [(i, i ^ 1 << bit) for i in range(count)])]
  transfers between devices with their start and end apart: 12 -> 51, of which waited for: 11 -> 23; matrix products, arithmetic and copies ran while one was open for 7% -> 8% of each run, Pallas kernels for 0% -> 43%
where the time goes in v1:
time: 320 us; the launch traced here: 315 us
  Pallas kernels  169 us (53%)
  starting transfers between devices  53.3 us (17%)
  waiting for transfers between devices  45.9 us (14%)
  local copies, waits for them, and re-layouts  20.4 us (6%)
  other arithmetic  17.2 us (5%)
  between operations  9.13 us (3%)
    pallas_call x17, Pallas kernels, call(): pl.pallas_call(kernel, out_shape=[pltpu.HBM(dims, dtype) if space == HBM...  169 us
    ppermute x38, starting transfers between devices, swap_bit(): return lax.ppermute(value, 'dp', [(i, i ^ 1 << bit) for i in range(count)])  49.4 us
    ppermute x38, waiting for transfers between devices, swap_bit(): return lax.ppermute(value, 'dp', [(i, i ^ 1 << bit) for i in range(count)])  34.7 us
    unnamed x83, local copies, waits for them, and re-layouts  13.7 us
    ppermute x13, waiting for transfers between devices, swap_cores(): return lax.ppermute(value, 'tensor', [(0, 1), (1, 0)])  11.2 us
  transfers between devices with their start and end apart: 51, of which 23 were waited for; matrix products, arithmetic and copies ran while one was open for 8% of the time, Pallas kernels for 43%

profile of v1, /device:TPU:0, one launch (start us, length us, event | category | flops | bytes accessed | tf_op | source)
XLA Modules:
  0.0 314.5 jit_solution(18126115107474092658)
XLA Ops:
  1.2 4.5 %collective-permute-done.wo_ref.ao_ref = bf16[4,768,384]{2,1,0:T(8,128)(2,1)} collective-permute-done((bf16[4,768,384]{2,1,0:T(8,128)(2,1)}, bf16[4,768,384]{2,1,0:T(8,128)(2,1)}, u32[]{:S(2)}, u32[]{:S(2)}) %collective-permute-start) | collective-permute-done | bytes 2359328 | tf_op jit(solution)/shard_map/ppermute | solution.py:758
  7.2 6.3 %collective-permute-done.1.bo_ref = f32[2,384]{1,0:T(2,128)S(1)} collective-permute-done((f32[2,384]{1,0:T(2,128)S(1)}, f32[2,384]{1,0:T(2,128)S(1)}, u32[]{:S(2)}, u32[]{:S(2)}) %collective-permute-start.1) | collective-permute-done | bytes 3104 | tf_op jit(solution)/shard_map/ppermute | solution.py:758
  14.2 21.4 %attention_forward.1 = (bf16[1024,768]{1,0:T(8,128)(2,1)}, bf16[1024,768]{1,0:T(8,128)(2,1)}, bf16[1024,768]{1,0:T(8,128)(2,1)}, bf16[1024,128]{1,0:T(8,128)(2,1...) custom-call(s32[1]{0:T(128)} %bitcast.core_ref, bf16[2048,768]{1,0:T(8,128)(2,1)} %frames_ref.7, ...), custom_call_target="tpu_custom_call" | custom-call | flops 15000000512 | bytes 20000000 | tf_op jit(solution)/shard_map/attention_forward/pallas_call | solution.py:59
  36.1 28.5 %ffn_forward.1 = (f32[1024,768]{1,0:T(8,128)}, f32[1024,128]{1,0:T(8,128)}, bf16[1024,768]{1,0:T(8,128)(2,1)}, bf16[1024,768]{1,0:T(8,128)(2,1)}, f32[1024,768]{...) custom-call(s32[1]{0:T(128)} %bitcast.core_ref, ...), custom_call_target="tpu_custom_call" | custom-call | flops 15699999744 | bytes 40000000 | tf_op jit(solution)/shard_map/ffn_forward/pallas_call | solution.py:59
  64.8 18.5 %hidden_backward.1 = (bf16[1024,3072]{1,0:T(8,128)(2,1)}, bf16[3,768,512]{2,1,0:T(8,128)(2,1)}, bf16[3,768,512]{2,1,0:T(8,128)(2,1)}, f32[1,1536]{1,0:T(1,128)}, f32[1,1536]{1,0:T(1,128)}) custom-call(bf16[1024,768]{1,0:T(8,128)(2,1)} %get-tuple-element.140.glow_ref, bf16[1024,3072]{1,0:T(8,128)(2,1)} %get-tuple-element.141.slope_ref, ...), custom_call_target="tpu_custom_call" | custom-call | flops 9699999744 | bytes 30000000 | tf_op jit(solution)/shard_map/hidden_backward/pallas_call | solution.py:59
  84.4 3.2 %fold.9 = (bf16[2,2,2,48,512]{4,3,2,1,0:T(8,128)(2,1)}, bf16[2,2,2,48,512]{4,3,2,1,0:T(8,128)(2,1)}, bf16[2,2,2,48,512]{4,3,2,1,0:T(8,128)(2,1)}) custom-call(s32[4]{0:T(128)} %pad_add_fusion.place_ref, bf16[3,2,2,2,2,48,512]{6,5,4,3,2,1,0:T(8,128)(2,1)} %bitcast.37, bf16[3,2,2,2,2,48,512]{6,5,4,3,2,1,0:T(8,128)(2,1)} %bitcast.8.refs_1_.refs_13_), custom_call_target="tpu_custom_call" | custom-call | flops 2359296 | bytes 7077888 | tf_op jit(solution)/shard_map/fold/pallas_call | solution.py:59
  87.6 18.4 %norm_backward.1 = (f32[1024,768]{1,0:T(8,128)}, bf16[3,768,128]{2,1,0:T(8,128)(2,1)}, bf16[3,768,128]{2,1,0:T(8,128)(2,1)}, bf16[1024,768]{1,0:T(8,128)(2,1)}, ...) custom-call(bf16[1024,3072]{1,0:T(8,128)(2,1)} %get-tuple-element.149.gup_ref, f32[1024,768]{1,0:T(8,128)} %get-tuple-element.150.g2_ref, ...), custom_call_target="tpu_custom_call" | custom-call | flops 7500000256 | bytes 30000000 | tf_op jit(solution)/shard_map/norm_backward/pallas_call | solution.py:59
  106.1 2.9 collective-permute-start.6
  109.0 2.6 collective-permute-start.7
  115.7 3.1 collective-permute-done.6.refs_2_.refs_14_
  122.4 4.4 %fold.10 = (bf16[2,2,48,512]{3,2,1,0:T(8,128)(2,1)}, bf16[2,2,48,512]{3,2,1,0:T(8,128)(2,1)}, bf16[2,2,48,512]{3,2,1,0:T(8,128)(2,1)}, bf16[2,2,2,48,640]{4,3,2,...) custom-call(s32[4]{0:T(128)} %pad_add_fusion.place_ref, ...), custom_call_target="tpu_custom_call" | custom-call | flops 4718592 | bytes 14155776 | tf_op jit(solution)/shard_map/fold/pallas_call | solution.py:59
  131.4 3.6 %collective-permute-done.11.refs_3_.refs_15_ = bf16[2,2,48,512]{3,2,1,0:T(8,128)(2,1)} collective-permute-done((bf16[2,2,48,512]{3,2,1,0:T(8,128)(2,1)}, bf16[2,2,48,512]{3,2,1,0:T(8,128)(2,1)}, u32[]{:S(2)}, u32[]{:S(2)}) %collective-permute-start.11) | collective-permute-done | bytes 196640 | tf_op jit(solution)/shard_map/ppermute | solution.py:762
  135.4 19.5 %heads_backward.2 = (bf16[1024,384]{1,0:T(8,128)(2,1)}, bf16[1024,384]{1,0:T(8,128)(2,1)}, bf16[1024,384]{1,0:T(8,128)(2,1)}, bf16[3,768,384]{2,1,0:T(8,128)(2,1)}, f32[8,384]{1,0:T(8,128)}) custom-call(s32[2,4]{1,0:T(2,128)} %get-tuple-element.131.win_ref, s32[1]{0:T(128)} %bitcast.core_ref, bf16[1024,768]{1,0:T(8,128)(2,1)} %get-tuple-element.132.q_ref, ...), custom_call_target="tpu_custom_call" | custom-call | flops 12000000000 | bytes 15000000 | tf_op jit(solution)/shard_map/heads_backward/pallas_call | solution.py:59
  157.6 3.8 %fold.11 = (bf16[2,48,512]{2,1,0:T(8,128)(2,1)}, bf16[2,48,512]{2,1,0:T(8,128)(2,1)}, bf16[2,48,512]{2,1,0:T(8,128)(2,1)}, bf16[2,2,48,640]{3,2,1,0:T(8,128)(2,1...) custom-call(s32[4]{0:T(128)} %pad_add_fusion.place_ref, ...), custom_call_target="tpu_custom_call" | custom-call | flops 3391488 | bytes 10174464 | tf_op jit(solution)/shard_map/fold/pallas_call | solution.py:59
  161.4 19.5 %heads_backward.3 = (bf16[1024,384]{1,0:T(8,128)(2,1)}, bf16[1024,384]{1,0:T(8,128)(2,1)}, bf16[1024,384]{1,0:T(8,128)(2,1)}, bf16[3,768,384]{2,1,0:T(8,128)(2,1)}, f32[8,384]{1,0:T(8,128)}) custom-call(s32[2,4]{1,0:T(2,128)} %get-tuple-element.131.win_ref, s32[1]{0:T(128)} %bitcast.core_ref, bf16[1024,768]{1,0:T(8,128)(2,1)} %get-tuple-element.132.q_ref, ...), custom_call_target="tpu_custom_call" | custom-call | flops 12000000000 | bytes 15000000 | tf_op jit(solution)/shard_map/heads_backward/pallas_call | solution.py:59
  192.7 9.5 %input_gradient.1 = bf16[1024,768]{1,0:T(8,128)(2,1)} custom-call(bf16[1024,384]{1,0:T(8,128)(2,1)} %get-tuple-element.179.qm_ref, bf16[1024,384]{1,0:T(8,128)(2,1)} %get-tuple-element.180.km_ref, bf16[1024,384]{1,0:T(8,128)(2,1)} %get-tuple-element.181.vm_ref, bf16[1024,384]{1,0:T(8,128)(2,1)} %get-tuple-element.182.qo_ref, ...), custom_call_target="tpu_custom_call" | custom-call | flops 3600000000 | bytes 15000000 | tf_op jit(solution)/shard_map/input_gradient/pallas_call | solution.py:59
  203.0 3.4 %collective-permute-start.23 = (f32[6912]{0:T(1024)S(1)}, f32[6912]{0:T(1024)S(1)}, u32[]{:S(2)}, u32[]{:S(2)}) collective-permute-start(f32[6912]{0:T(1024)S(1)} %add.69), channel_id=1, source_target_pairs={{0,16},{2,18},{4,20},{6,22},{8,24},{10,26},{12,28},{14,30},{16,0},... | collective-permute-start | bytes 82952 | tf_op jit(solution)/shard_map/ppermute | solution.py:762
  218.0 3.9 %fold.12 = (bf16[2,2,2,48,384]{4,3,2,1,0:T(8,128)(2,1)}, bf16[2,2,2,48,384]{4,3,2,1,0:T(8,128)(2,1)}, bf16[2,2,2,48,384]{4,3,2,1,0:T(8,128)(2,1)}, bf16[2,48,640...) custom-call(s32[4]{0:T(128)} %pad_add_fusion.place_ref, ...), custom_call_target="tpu_custom_call" | custom-call | flops 3981312 | bytes 11943936 | tf_op jit(solution)/shard_map/fold/pallas_call | solution.py:59
  231.4 3.9 %collective-permute-done.37.refs_17_.refs_25_ = bf16[2,48,640]{2,1,0:T(8,128)(2,1)S(1)} collective-permute-done((bf16[2,48,640]{2,1,0:T(8,128)(2,1)}, bf16[2,48,640]{2,1,0:T(8,128)(2,1)S(1)}, u32[]{:S(2)}, u32[]{:S(2)}) %collective-permute-start.37) | collective-permute-done | bytes 122912 | tf_op jit(solution)/shard_map/ppermute | solution.py:762
  236.7 3.3 %fold.13 = (bf16[2,2,48,384]{3,2,1,0:T(8,128)(2,1)}, bf16[2,2,48,384]{3,2,1,0:T(8,128)(2,1)}, bf16[2,2,48,384]{3,2,1,0:T(8,128)(2,1)}, bf16[3,48,640]{2,1,0:T(8,128)(2,1)}) custom-call(s32[4]{0:T(128)} %pad_add_fusion.place_ref, bf16[3,2,2,2,2,48,384]{6,5,4,3,2,1,0:T(8,128)(2,1)} %bitcast.48, bf16[3,2,2,2,2,48,384]{6,5,4,3,2,1,0:T(8,128)(2,1)} %bitcast.15.refs_1_, ...), custom_call_target="tpu_custom_call" | custom-call | flops 2248704 | bytes 6746112 | tf_op jit(solution)/shard_map/fold/pallas_call | solution.py:59
  248.5 2.7 fold.15
  254.3 3.7 %broadcast_select_fusion.1 = (bf16[1024,768]{1,0:T(8,128)(2,1)}, bf16[1024,768]{1,0:T(8,128)(2,1)}) fusion(bf16[1024,768]{1,0:T(8,128)(2,1)} %input_gradient.1, bf16[1024,768]{1,0:T(8,128)(2,1)} %collective-permute-done.17, pred[]{:T(512)S(6)} %eq.2), kind=kLoop, calls=%fused_computation.3 | loop fusion | flops 1572864 | bytes 6291457 | tf_op jit(solution)/shard_map/jit(_where)/select_n | solution.py:1093
  262.2 2.5 fold.16
  265.7 5.1 %maximum_convert_fusion = f32[2048,768]{1,0:T(8,128)} fusion(bf16[1024,768]{1,0:T(8,128)(2,1)} %get-tuple-element.253, bf16[1024,768]{1,0:T(8,128)(2,1)} %get-tuple-element.252), kind=kLoop, calls=%fused_computation.1 | loop fusion | flops 6291456 | bytes 9437184 | tf_op jit(solution)/shard_map/convert_element_type | solution.py:1099
  271.9 2.5 collective-permute-done.38.refs_19_
  275.1 4.2 %fold.14 = (f32[3,48,512]{2,1,0:T(8,128)}, f32[3,48,640]{2,1,0:T(8,128)}, f32[1,1]{1,0:T(1,128)}) custom-call(s32[4]{0:T(128)} %pad_add_fusion.place_ref, bf16[3,2,2,2,2,48,512]{6,5,4,3,2,1,0:T(8,128)(2,1)} %bitcast.41, bf16[3,2,2,2,2,48,512]{6,5,4,3,2,1,0:T(8,128)(2,1)} %bitcast.8.refs_1_.refs_13_, bf16[2,2,2,48,512]{4,3,2,1,0:T(8,128)(2,1)} %copy-done.14, ...), custom_call_target="tpu_custom_call" | custom-call | flops 1990656 | bytes 5971968 | tf_op jit(solution)/shard_map/fold/pallas_call | solution.py:59
  280.7 3.3 %fold.17 = (f32[3,48,384]{2,1,0:T(8,128)}, f32[1,1]{1,0:T(1,128)}) custom-call(s32[4]{0:T(128)} %pad_add_fusion.place_ref, bf16[3,2,2,2,2,48,384]{6,5,4,3,2,1,0:T(8,128)(2,1)} %bitcast.51, bf16[3,2,2,2,2,48,384]{6,5,4,3,2,1,0:T(8,128)(2,1)} %bitcast.15.refs_1_, bf16[2,2,2,48,384]{4,3,2,1,0:T(8,128)(2,1)} %copy-done.15, bf16[2,2,48,384]{3,2,1,0:T(8,128)(2,1)} %copy-done.18, ...), custom_call_target="tpu_custom_call" | custom-call | flops 663552 | bytes 1990656 | tf_op jit(solution)/shard_map/fold/pallas_call | solution.py:59
  286.6 2.2 collective-permute-start.47
  290.9 2.3 collective-permute-start.48
  296.6 2.3 collective-permute-done.49
  301.0 3.2 %collective-permute-done.50 = f32[1,1]{1,0:T(1,128)} collective-permute-done((f32[1,1]{1,0:T(1,128)}, f32[1,1]{1,0:T(1,128)}, u32[]{:S(2)}, u32[]{:S(2)}) %collective-permute-start.50) | collective-permute-done | bytes 36 | tf_op jit(solution)/shard_map/ppermute | solution.py:762
  311.0 2.2 update.1
  (206 shorter events, 84.9 us)
Async XLA Ops:
  5.7 29.9 %collective-permute-start.2 = (bf16[2,768,1536]{2,1,0:T(8,128)(2,1)}, bf16[2,768,1536]{2,1,0:T(8,128)(2,1)}, u32[]{:S(2)}, u32[]{:S(2)}) collective-permute-start(bf16[2,768,1536]{2,1,0:T(8,128)(2,1)} %fm_ref.5), channel_id=1, source_target_pairs={{0,1},{1,0},{2,3},{3,2},{4,5},{5,4},{6,7},{7,6},{8,9},{9,8},{10,11... | collective-permute-start | bytes 14155784 | tf_op jit(solution)/shard_map/ppermute | solution.py:758
  6.9 28.7 %collective-permute-start.3 = (f32[1,1536]{1,0:T(1,128)}, f32[1,1536]{1,0:T(1,128)S(1)}, u32[]{:S(2)}, u32[]{:S(2)}) collective-permute-start(f32[1,1536]{1,0:T(1,128)} %hm_ref.1), channel_id=1, source_target_pairs={{0,1},{1,0},{2,3},{3,2},{4,5},{5,4},{6,7},{7,6},{8,9},{9,8},{10,11... | collective-permute-start | bytes 18440 | tf_op jit(solution)/shard_map/ppermute | solution.py:758
  64.7 19.7 %collective-permute-start.5 = (bf16[3,768,512]{2,1,0:T(8,128)(2,1)}, bf16[3,768,512]{2,1,0:T(8,128)(2,1)}, u32[]{:S(2)}, u32[]{:S(2)}) collective-permute-start(bf16[3,768,512]{2,1,0:T(8,128)(2,1)} %get-tuple-element.136), channel_id=1, source_target_pairs={{0,1},{1,0},{2,3},{3,2},{4,5},{5,4},{6,7},{7,6},{8,9},{9,8},{10,11... | collective-permute-start | bytes 7077896 | tf_op jit(solution)/shard_map/ppermute | solution.py:758
  83.2 31.6 %collective-permute-start.9 = (bf16[3,768,512]{2,1,0:T(8,128)(2,1)}, bf16[3,768,512]{2,1,0:T(8,128)(2,1)}, u32[]{:S(2)}, u32[]{:S(2)}) collective-permute-start(bf16[3,768,512]{2,1,0:T(8,128)(2,1)} %get-tuple-element.148), channel_id=1, source_target_pairs={{0,1},{1,0},{2,3},{3,2},{4,5},{5,4},{6,7},{7,6},{8,9},{9,8},{10,11... | collective-permute-start | bytes 7077896 | tf_op jit(solution)/shard_map/ppermute | solution.py:758
  106.0 16.5 %collective-permute-start.10 = (bf16[3,768,128]{2,1,0:T(8,128)(2,1)}, bf16[3,768,128]{2,1,0:T(8,128)(2,1)}, u32[]{:S(2)}, u32[]{:S(2)}) collective-permute-start(bf16[3,768,128]{2,1,0:T(8,128)(2,1)} %get-tuple-element.154), channel_id=1, source_target_pairs={{0,1},{1,0},{2,3},{3,2},{4,5},{5,4},{6,7},{7,6},{8,9},{9,8},{10,11... | collective-permute-start | bytes 1769480 | tf_op jit(solution)/shard_map/ppermute | solution.py:758
  106.1 12.8 %collective-permute-start.6 = (bf16[2,2,2,48,512]{4,3,2,1,0:T(8,128)(2,1)}, bf16[2,2,2,48,512]{4,3,2,1,0:T(8,128)(2,1)S(1)}, u32[]{:S(2)}, u32[]{:S(2)}) collective-permute-start(bf16[2,2,2,48,512]{4,3,2,1,0:T(8,128)(2,1)} %get-tuple-element.144), channel_id=1, source_target_pairs={{0,2},{2,0},{4,6},{6,4},{8,10},{10,8},{12,14},{14,12},{16,18},{18,... | collective-permute-start | bytes 1179656 | tf_op jit(solution)/shard_map/ppermute | solution.py:762
  109.0 12.0 %collective-permute-start.7 = (bf16[2,2,2,48,512]{4,3,2,1,0:T(8,128)(2,1)}, bf16[2,2,2,48,512]{4,3,2,1,0:T(8,128)(2,1)}, u32[]{:S(2)}, u32[]{:S(2)}) collective-permute-start(bf16[2,2,2,48,512]{4,3,2,1,0:T(8,128)(2,1)} %get-tuple-element.145), channel_id=1, source_target_pairs={{0,4},{2,6},{4,0},{6,2},{8,12},{10,14},{12,8},{14,10},{16,20},{18,... | collective-permute-start | bytes 1179656 | tf_op jit(solution)/shard_map/ppermute | solution.py:762
  111.6 10.9 %collective-permute-start.8 = (bf16[2,2,2,48,512]{4,3,2,1,0:T(8,128)(2,1)}, bf16[2,2,2,48,512]{4,3,2,1,0:T(8,128)(2,1)}, u32[]{:S(2)}, u32[]{:S(2)}) collective-permute-start(bf16[2,2,2,48,512]{4,3,2,1,0:T(8,128)(2,1)} %get-tuple-element.146), channel_id=1, source_target_pairs={{0,8},{2,10},{4,12},{6,14},{8,0},{10,2},{12,4},{14,6},{16,24},{18,... | collective-permute-start | bytes 1179656 | tf_op jit(solution)/shard_map/ppermute | solution.py:762
  114.8 12.8 %collective-permute-start.19 = (f32[6,768]{1,0:T(8,128)S(1)}, f32[6,768]{1,0:T(8,128)S(1)}, u32[]{:S(2)}, u32[]{:S(2)}) collective-permute-start(f32[6,768]{1,0:T(8,128)S(1)} %pad_maximum_fusion.2), channel_id=1, source_target_pairs={{0,1},{1,0},{2,3},{3,2},{4,5},{5,4},{6,7},{7,6},{8,9},{9,8},{10,11... | collective-permute-start | bytes 55304 | tf_op jit(solution)/shard_map/ppermute | solution.py:758
  126.9 8.2 %collective-permute-start.11 = (bf16[2,2,48,512]{3,2,1,0:T(8,128)(2,1)}, bf16[2,2,48,512]{3,2,1,0:T(8,128)(2,1)}, u32[]{:S(2)}, u32[]{:S(2)}) collective-permute-start(bf16[2,2,48,512]{3,2,1,0:T(8,128)(2,1)} %get-tuple-element.162), channel_id=1, source_target_pairs={{0,4},{2,6},{4,0},{6,2},{8,12},{10,14},{12,8},{14,10},{16,20},{18,... | collective-permute-start | bytes 589832 | tf_op jit(solution)/shard_map/ppermute | solution.py:762
  127.6 29.1 %collective-permute-start.14 = (bf16[2,2,2,48,640]{4,3,2,1,0:T(8,128)(2,1)}, bf16[2,2,2,48,640]{4,3,2,1,0:T(8,128)(2,1)S(1)}, u32[]{:S(2)}, u32[]{:S(2)}) collective-permute-start(bf16[2,2,2,48,640]{4,3,2,1,0:T(8,128)(2,1)} %get-tuple-element.165), channel_id=1, source_target_pairs={{0,2},{2,0},{4,6},{6,4},{8,10},{10,8},{12,14},{14,12},{16,18},{18,... | collective-permute-start | bytes 1474568 | tf_op jit(solution)/shard_map/ppermute | solution.py:762
  128.3 28.5 %collective-permute-start.15 = (bf16[2,2,2,48,640]{4,3,2,1,0:T(8,128)(2,1)}, bf16[2,2,2,48,640]{4,3,2,1,0:T(8,128)(2,1)}, u32[]{:S(2)}, u32[]{:S(2)}) collective-permute-start(bf16[2,2,2,48,640]{4,3,2,1,0:T(8,128)(2,1)} %get-tuple-element.166), channel_id=1, source_target_pairs={{0,4},{2,6},{4,0},{6,2},{8,12},{10,14},{12,8},{14,10},{16,20},{18,... | collective-permute-start | bytes 1474568 | tf_op jit(solution)/shard_map/ppermute | solution.py:762
  129.4 27.4 %collective-permute-start.16 = (bf16[2,2,2,48,640]{4,3,2,1,0:T(8,128)(2,1)}, bf16[2,2,2,48,640]{4,3,2,1,0:T(8,128)(2,1)}, u32[]{:S(2)}, u32[]{:S(2)}) collective-permute-start(bf16[2,2,2,48,640]{4,3,2,1,0:T(8,128)(2,1)} %get-tuple-element.167), channel_id=1, source_target_pairs={{0,8},{2,10},{4,12},{6,14},{8,0},{10,2},{12,4},{14,6},{16,24},{18,... | collective-permute-start | bytes 1474568 | tf_op jit(solution)/shard_map/ppermute | solution.py:762
  130.9 25.3 %collective-permute-start.12 = (bf16[2,2,48,512]{3,2,1,0:T(8,128)(2,1)}, bf16[2,2,48,512]{3,2,1,0:T(8,128)(2,1)}, u32[]{:S(2)}, u32[]{:S(2)}) collective-permute-start(bf16[2,2,48,512]{3,2,1,0:T(8,128)(2,1)} %get-tuple-element.163), channel_id=1, source_target_pairs={{0,8},{2,10},{4,12},{6,14},{8,0},{10,2},{12,4},{14,6},{16,24},{18,... | collective-permute-start | bytes 589832 | tf_op jit(solution)/shard_map/ppermute | solution.py:762
  135.1 21.2 %collective-permute-start.13 = (bf16[2,2,48,512]{3,2,1,0:T(8,128)(2,1)}, bf16[2,2,48,512]{3,2,1,0:T(8,128)(2,1)}, u32[]{:S(2)}, u32[]{:S(2)}) collective-permute-start(bf16[2,2,48,512]{3,2,1,0:T(8,128)(2,1)} %get-tuple-element.164), channel_id=1, source_target_pairs={{0,2},{2,0},{4,6},{6,4},{8,10},{10,8},{12,14},{14,12},{16,18},{18,... | collective-permute-start | bytes 589832 | tf_op jit(solution)/shard_map/ppermute | solution.py:762
  156.3 46.7 %collective-permute-start.4 = (bf16[1024,768]{1,0:T(8,128)(2,1)}, bf16[1024,768]{1,0:T(8,128)(2,1)}, u32[]{:S(2)}, u32[]{:S(2)}) collective-permute-start(bf16[1024,768]{1,0:T(8,128)(2,1)} %get-tuple-element.130), channel_id=1, source_target_pairs={{0,1},{1,0},{2,3},{3,2},{4,5},{5,4},{6,7},{7,6},{8,9},{9,8},{10,11... | collective-permute-start | bytes 4718600 | tf_op jit(solution)/shard_map/ppermute | solution.py:758
  156.3 25.4 %collective-permute-start.18 = (f32[2304]{0:T(1024)}, f32[2304]{0:T(1024)}, u32[]{:S(2)}, u32[]{:S(2)}) collective-permute-start(f32[2304]{0:T(1024)} %pad_maximum_fusion.3), channel_id=1, source_target_pairs={{0,1},{1,0},{2,3},{3,2},{4,5},{5,4},{6,7},{7,6},{8,9},{9,8},{10,11... | collective-permute-start | bytes 27656 | tf_op jit(solution)/shard_map/ppermute | solution.py:758
  180.9 36.6 %collective-permute-start.25 = (bf16[3,768,384]{2,1,0:T(8,128)(2,1)}, bf16[3,768,384]{2,1,0:T(8,128)(2,1)}, u32[]{:S(2)}, u32[]{:S(2)}) collective-permute-start(bf16[3,768,384]{2,1,0:T(8,128)(2,1)} %get-tuple-element.194), channel_id=1, source_target_pairs={{0,1},{1,0},{2,3},{3,2},{4,5},{5,4},{6,7},{7,6},{8,9},{9,8},{10,11... | collective-permute-start | bytes 5308424 | tf_op jit(solution)/shard_map/ppermute | solution.py:758
  187.9 15.1 %collective-permute-start.24 = (bf16[2,48,512]{2,1,0:T(8,128)(2,1)}, bf16[2,48,512]{2,1,0:T(8,128)(2,1)S(1)}, u32[]{:S(2)}, u32[]{:S(2)}) collective-permute-start(bf16[2,48,512]{2,1,0:T(8,128)(2,1)} %get-tuple-element.192), channel_id=1, source_target_pairs={{0,8},{2,10},{4,12},{6,14},{8,0},{10,2},{12,4},{14,6},{16,24},{18,... | collective-permute-start | bytes 294920 | tf_op jit(solution)/shard_map/ppermute | solution.py:762
  190.1 18.4 %collective-permute-start.29 = (bf16[2,48,512]{2,1,0:T(8,128)(2,1)S(1)}, bf16[2,48,512]{2,1,0:T(8,128)(2,1)}, u32[]{:S(2)}, u32[]{:S(2)}) collective-permute-start(bf16[2,48,512]{2,1,0:T(8,128)(2,1)S(1)} %copy-done.38), channel_id=1, source_target_pairs={{0,2},{2,0},{4,6},{6,4},{8,10},{10,8},{12,14},{14,12},{16,18},{18,... | collective-permute-start | bytes 294920 | tf_op jit(solution)/shard_map/ppermute | solution.py:762
  191.2 11.1 %collective-permute-start.22 = (f32[6912]{0:T(1024)S(1)}, f32[6912]{0:T(1024)S(1)}, u32[]{:S(2)}, u32[]{:S(2)}) collective-permute-start(f32[6912]{0:T(1024)S(1)} %add.68), channel_id=1, source_target_pairs={{0,8},{2,10},{4,12},{6,14},{8,0},{10,2},{12,4},{14,6},{16,24},{18,... | collective-permute-start | bytes 82952 | tf_op jit(solution)/shard_map/ppermute | solution.py:762
  202.9 51.3 %collective-permute-start.17 = (bf16[1024,768]{1,0:T(8,128)(2,1)}, bf16[1024,768]{1,0:T(8,128)(2,1)}, u32[]{:S(2)}, u32[]{:S(2)}) collective-permute-start(bf16[1024,768]{1,0:T(8,128)(2,1)} %input_gradient.1), channel_id=1, source_target_pairs={{0,1},{1,0},{2,3},{3,2},{4,5},{5,4},{6,7},{7,6},{8,9},{9,8},{10,11... | collective-permute-start | bytes 4718600 | tf_op jit(solution)/shard_map/ppermute | solution.py:758
  208.6 8.1 %collective-permute-start.26 = (bf16[2,2,48,640]{3,2,1,0:T(8,128)(2,1)S(1)}, bf16[2,2,48,640]{3,2,1,0:T(8,128)(2,1)S(1)}, u32[]{:S(2)}, u32[]{:S(2)}) collective-permute-start(bf16[2,2,48,640]{3,2,1,0:T(8,128)(2,1)S(1)} %copy-done.36), channel_id=1, source_target_pairs={{0,4},{2,6},{4,0},{6,2},{8,12},{10,14},{12,8},{14,10},{16,20},{18,... | collective-permute-start | bytes 737288 | tf_op jit(solution)/shard_map/ppermute | solution.py:762
  209.6 7.8 %collective-permute-start.28 = (bf16[2,2,48,640]{3,2,1,0:T(8,128)(2,1)S(1)}, bf16[2,2,48,640]{3,2,1,0:T(8,128)(2,1)}, u32[]{:S(2)}, u32[]{:S(2)}) collective-permute-start(bf16[2,2,48,640]{3,2,1,0:T(8,128)(2,1)S(1)} %copy-done.34), channel_id=1, source_target_pairs={{0,2},{2,0},{4,6},{6,4},{8,10},{10,8},{12,14},{14,12},{16,18},{18,... | collective-permute-start | bytes 737288 | tf_op jit(solution)/shard_map/ppermute | solution.py:762
  224.6 10.7 %collective-permute-start.33 = (bf16[2,2,2,48,384]{4,3,2,1,0:T(8,128)(2,1)}, bf16[2,2,2,48,384]{4,3,2,1,0:T(8,128)(2,1)S(1)}, u32[]{:S(2)}, u32[]{:S(2)}) collective-permute-start(bf16[2,2,2,48,384]{4,3,2,1,0:T(8,128)(2,1)} %get-tuple-element.202), channel_id=1, source_target_pairs={{0,2},{2,0},{4,6},{6,4},{8,10},{10,8},{12,14},{14,12},{16,18},{18,... | collective-permute-start | bytes 884744 | tf_op jit(solution)/shard_map/ppermute | solution.py:762
  225.8 10.3 %collective-permute-start.34 = (bf16[2,2,2,48,384]{4,3,2,1,0:T(8,128)(2,1)}, bf16[2,2,2,48,384]{4,3,2,1,0:T(8,128)(2,1)}, u32[]{:S(2)}, u32[]{:S(2)}) collective-permute-start(bf16[2,2,2,48,384]{4,3,2,1,0:T(8,128)(2,1)} %get-tuple-element.203), channel_id=1, source_target_pairs={{0,4},{2,6},{4,0},{6,2},{8,12},{10,14},{12,8},{14,10},{16,20},{18,... | collective-permute-start | bytes 884744 | tf_op jit(solution)/shard_map/ppermute | solution.py:762
  227.0 9.0 %collective-permute-start.35 = (bf16[2,2,2,48,384]{4,3,2,1,0:T(8,128)(2,1)}, bf16[2,2,2,48,384]{4,3,2,1,0:T(8,128)(2,1)}, u32[]{:S(2)}, u32[]{:S(2)}) collective-permute-start(bf16[2,2,2,48,384]{4,3,2,1,0:T(8,128)(2,1)} %get-tuple-element.204), channel_id=1, source_target_pairs={{0,8},{2,10},{4,12},{6,14},{8,0},{10,2},{12,4},{14,6},{16,24},{18,... | collective-permute-start | bytes 884744 | tf_op jit(solution)/shard_map/ppermute | solution.py:762
  251.2 9.8 %collective-permute-start.42 = (bf16[2,48,384]{2,1,0:T(8,128)(2,1)}, bf16[2,48,384]{2,1,0:T(8,128)(2,1)S(1)}, u32[]{:S(2)}, u32[]{:S(2)}) collective-permute-start(bf16[2,48,384]{2,1,0:T(8,128)(2,1)} %get-tuple-element.212), channel_id=1, source_target_pairs={{0,8},{2,10},{4,12},{6,14},{8,0},{10,2},{12,4},{14,6},{16,24},{18,... | collective-permute-start | bytes 221192 | tf_op jit(solution)/shard_map/ppermute | solution.py:762
  252.0 8.9 %collective-permute-start.43 = (bf16[2,48,384]{2,1,0:T(8,128)(2,1)}, bf16[2,48,384]{2,1,0:T(8,128)(2,1)S(1)}, u32[]{:S(2)}, u32[]{:S(2)}) collective-permute-start(bf16[2,48,384]{2,1,0:T(8,128)(2,1)} %get-tuple-element.213), channel_id=1, source_target_pairs={{0,2},{2,0},{4,6},{6,4},{8,10},{10,8},{12,14},{14,12},{16,18},{18,... | collective-permute-start | bytes 221192 | tf_op jit(solution)/shard_map/ppermute | solution.py:762
  258.0 13.9 %collective-permute-start.31 = (bf16[3,48,512]{2,1,0:T(8,128)(2,1)}, bf16[3,48,512]{2,1,0:T(8,128)(2,1)}, u32[]{:S(2)}, u32[]{:S(2)}) collective-permute-start(bf16[3,48,512]{2,1,0:T(8,128)(2,1)} %get-tuple-element.200), channel_id=1, source_target_pairs={{0,16},{2,18},{4,20},{6,22},{8,24},{10,26},{12,28},{14,30},{16,0},... | collective-permute-start | bytes 442376 | tf_op jit(solution)/shard_map/ppermute | solution.py:762
  258.9 15.5 %collective-permute-start.38 = (bf16[3,48,640]{2,1,0:T(8,128)(2,1)}, bf16[3,48,640]{2,1,0:T(8,128)(2,1)S(1)}, u32[]{:S(2)}, u32[]{:S(2)}) collective-permute-start(bf16[3,48,640]{2,1,0:T(8,128)(2,1)} %get-tuple-element.207), channel_id=1, source_target_pairs={{0,16},{2,18},{4,20},{6,22},{8,24},{10,26},{12,28},{14,30},{16,0},... | collective-permute-start | bytes 552968 | tf_op jit(solution)/shard_map/ppermute | solution.py:762
  264.7 15.3 %collective-permute-start.45 = (bf16[3,48,384]{2,1,0:T(8,128)(2,1)}, bf16[3,48,384]{2,1,0:T(8,128)(2,1)S(1)}, u32[]{:S(2)}, u32[]{:S(2)}) collective-permute-start(bf16[3,48,384]{2,1,0:T(8,128)(2,1)} %fold.16), channel_id=1, source_target_pairs={{0,16},{2,18},{4,20},{6,22},{8,24},{10,26},{12,28},{14,30},{16,0},... | collective-permute-start | bytes 331784 | tf_op jit(solution)/shard_map/ppermute | solution.py:762
  (60 other events, 470.7 us)
